TPU v7x, 128 devices: a whole 4x4x4 slice. The times are simulated.
128 devices in a mesh: dp: 4 (over x_lo, core), expert: 32 (over z, y, x_hi).
Axes of the slice: x: 4 (x_hi: 2, x_lo: 2; x = x_hi * 2 + x_lo), y: 4, z: 4, core: 2. Of those that a mesh axis runs over, the one named last changes fastest.
Arguments:
- tokens: bfloat16 [16384, 5120], P(('dp', 'expert')), may hold values from -6 to 6
- router: bfloat16 [5120, 160], replicated, may hold values from -0.078125 to 0.078125
- expert_ids: int32 [16384, 6], P(('dp', 'expert')), may hold values from 0 to 31, all different within a row
- w_up: bfloat16 [32, 5120, 768], P('expert'), may hold values from -0.078125 to 0.078125
- w_down: bfloat16 [32, 768, 5120], P('expert'), may hold values from -0.21650635 to 0.21650635
- readout: bfloat16 [16384, 5120], P(('dp', 'expert')), may hold values from -0.078125 to 0.078125
- ref_logp: float32 [16384], P(('dp', 'expert')), may hold values from -3 to 3
- labels: int32 [128], P(('dp', 'expert')), may hold values 0 or 1
- prompt_read: bfloat16 [128, 5120], P(('dp', 'expert')), may hold values from -0.0074115883 to 0.0074115883
- kl_pair: int32 [128], P(('dp', 'expert')), may hold values from 0 to 31, as said below
- kl_ref: float32 [128], P(('dp', 'expert')), may hold values from 0 to 72
Outputs:
- grad_up: bfloat16 [32, 5120, 768], P('expert', 'dp')
- grad_down: bfloat16 [32, 768, 5120], P('expert', None, 'dp')
- losses: float32 [128], P(('dp', 'expert'))
- kl_terms: float32 [128], P(('dp', 'expert'))
Inputs may be any that keep to these rules, and one draw needn't show every extreme that they name: `expert_ids`: each row names 6 different experts. `kl_pair`: the position, among the 32 examples of the example's own data-parallel group, of another example of that group; never the example's own position.
All inputs are finite; a program needn't handle non-finite values. No bound on the sum of `labels` on one device may be relied on, other than what follows from the above.
Results may differ from a plain program's by a relative error of at most 0.015.
Values may be sent and summed in bfloat16 or wider, within the bound.
A program may use at most 192 MiB of HBM per device.

v0:
```python
import jax
import jax.numpy as jnp
from jax import lax
from jax.sharding import PartitionSpec as P

routed_scale = 16.0
kto_beta = 0.1
loss_scale = 1024.0


def silu_slope(pre_act):
    logistic = jax.nn.sigmoid(pre_act)
    return logistic * (1.0 + pre_act * (1.0 - logistic))


def contract_rows(left, right):
    return lax.dot_general(
        left, right, (((0,), (0,)), ((), ())), preferred_element_type=jnp.float32
    )


def local(
    tokens,
    router,
    expert_ids,
    w_up,
    w_down,
    readout,
    ref_logp,
    labels,
    prompt_read,
    kl_pair,
    kl_ref,
):
    experts_axis = lax.axis_size("expert")
    replicas = lax.axis_size("dp")
    tok_rows, model_width = tokens.shape
    top_count = expert_ids.shape[1]
    experts = experts_axis * w_up.shape[0]
    capacity = 4 * tok_rows * top_count // (5 * experts)
    up_matrix = w_up[0]
    down_matrix = w_down[0]
    seq_count = labels.shape[0]
    seq_len = tok_rows // seq_count
    slot_rows = experts * capacity
    logits = jnp.dot(tokens, router, preferred_element_type=jnp.float32)
    scores = jnp.exp(logits)
    router_probs = scores / jnp.sum(scores, axis=1, keepdims=True)
    gate_values = routed_scale * jnp.take_along_axis(router_probs, expert_ids, axis=1)
    onehot = (expert_ids[:, :, None] == jnp.arange(experts, dtype=jnp.int32)[None, None, :]).astype(
        jnp.int32
    )
    per_token = jnp.sum(onehot, axis=1)
    before = jnp.cumsum(per_token, axis=0) - per_token
    slot_rank = jnp.sum(onehot * before[:, None, :], axis=2)
    slot_index = jnp.where(slot_rank < capacity, expert_ids * capacity + slot_rank, slot_rows)
    outgoing = jnp.zeros((slot_rows, model_width), jnp.bfloat16)
    for column in range(top_count):
        outgoing = outgoing.at[slot_index[:, column]].set(tokens, mode="drop")
    outgoing = outgoing.reshape(experts, capacity, model_width)
    arrived = lax.all_to_all(outgoing, "expert", split_axis=0, concat_axis=0, tiled=True)
    slot_inputs = arrived.reshape(slot_rows, model_width)
    pre_act = jnp.dot(slot_inputs, up_matrix, preferred_element_type=jnp.float32)
    hidden = jax.nn.silu(pre_act).astype(jnp.bfloat16)
    expert_out = jnp.dot(hidden, down_matrix, preferred_element_type=jnp.float32).astype(
        jnp.bfloat16
    )
    returned = lax.all_to_all(
        expert_out.reshape(experts, capacity, model_width),
        "expert",
        split_axis=0,
        concat_axis=0,
        tiled=True,
    )
    returned_rows = jnp.concatenate(
        [returned.reshape(slot_rows, model_width), jnp.zeros((1, model_width), jnp.bfloat16)],
        axis=0,
    )
    routed_sum = jnp.zeros((tok_rows, model_width), jnp.float32)
    for column in range(top_count):
        routed_sum = routed_sum + gate_values[:, column : column + 1] * returned_rows[
            slot_index[:, column]
        ].astype(jnp.float32)
    layer_out = tokens.astype(jnp.float32) + routed_sum
    token_terms = jnp.sum(layer_out * readout.astype(jnp.float32), axis=1) - ref_logp
    margins = jnp.sum(token_terms.reshape(seq_count, seq_len), axis=1)
    seq_sums = jnp.sum(layer_out.reshape(seq_count, seq_len, model_width), axis=1)
    group_sums = lax.all_gather(seq_sums, "expert", axis=0, tiled=True)
    kl_terms = jnp.sum(group_sums[kl_pair] * prompt_read.astype(jnp.float32), axis=1) - kl_ref
    kl_total = lax.psum(jnp.sum(kl_terms), ("dp", "expert"))
    anchor = kl_total / (seq_count * experts_axis * replicas)
    signed = jnp.where(labels == 1, 1.0, -1.0)
    kept_share = jax.nn.sigmoid(kto_beta * signed * (margins - anchor))
    losses = 1.0 - kept_share
    margin_grad = -loss_scale * kto_beta * signed * kept_share * (1.0 - kept_share)
    grad_layer = jnp.repeat(margin_grad, seq_len)[:, None] * readout.astype(jnp.float32)
    grad_slots = jnp.zeros((slot_rows, model_width), jnp.bfloat16)
    for column in range(top_count):
        grad_slots = grad_slots.at[slot_index[:, column]].set(
            (gate_values[:, column : column + 1] * grad_layer).astype(jnp.bfloat16), mode="drop"
        )
    arrived_grads = lax.all_to_all(
        grad_slots.reshape(experts, capacity, model_width),
        "expert",
        split_axis=0,
        concat_axis=0,
        tiled=True,
    )
    slot_grad = arrived_grads.reshape(slot_rows, model_width)
    back = lax.dot_general(
        slot_grad, down_matrix, (((1,), (1,)), ((), ())), preferred_element_type=jnp.float32
    )
    pre_grad = (back * silu_slope(pre_act)).astype(jnp.bfloat16)
    up_part = contract_rows(slot_inputs, pre_grad)
    down_part = contract_rows(hidden, slot_grad)
    up_total, down_total = (
        lax.psum_scatter(
            up_part.astype(jnp.bfloat16), "dp", scatter_dimension=0, tiled=True
        ).astype(jnp.float32),
        lax.psum_scatter(
            down_part.astype(jnp.bfloat16), "dp", scatter_dimension=1, tiled=True
        ).astype(jnp.float32),
    )
    grad_up = up_total.astype(jnp.bfloat16)[None]
    grad_down = down_total.astype(jnp.bfloat16)[None]
    return (grad_up, grad_down, losses, kl_terms)


def solution(mesh):
    return jax.shard_map(
        local,
        mesh=mesh,
        in_specs=(
            P(("dp", "expert"), None),
            P(),
            P(("dp", "expert"), None),
            P("expert", None, None),
            P("expert", None, None),
            P(("dp", "expert"), None),
            P(("dp", "expert")),
            P(("dp", "expert")),
            P(("dp", "expert"), None),
            P(("dp", "expert")),
            P(("dp", "expert")),
        ),
        out_specs=(
            P("expert", "dp", None),
            P("expert", None, "dp"),
            P(("dp", "expert")),
            P(("dp", "expert")),
        ),
        check_vma=False,
    )
```

profile of v0, /device:TPU:1, one launch (start us, length us, event | category | flops | bytes accessed | tf_op | source)
XLA Modules:
  0.0 892.8 jit_solution(3442472078123971652)
XLA Ops:
  16.8 9.4 %scatter_fusion = bf16[608,5120]{1,0:T(8,128)(2,1)} fusion(bf16[608,5120]{1,0:T(8,128)(2,1)} %scatter_custom_fusion, s32[128]{0:T(128)S(1)} %get-tuple-element.25, bf16[128,5120]{1,0:T(8,128)(2,1)S(1)} %copy-done.2), kind=kCustom, calls=%fused_computation.8 | custom fusion | bytes 3932672 | tf_op jit(solution)/shard_map/scatter | solution.py:59
  26.3 9.0 %scatter_fusion.1 = bf16[608,5120]{1,0:T(8,128)(2,1)} fusion(bf16[608,5120]{1,0:T(8,128)(2,1)} %scatter_fusion, s32[128]{0:T(128)S(1)} %get-tuple-element.26, bf16[128,5120]{1,0:T(8,128)(2,1)S(1)} %copy-done.2), kind=kCustom, calls=%fused_computation.9 | custom fusion | bytes 3932672 | tf_op jit(solution)/shard_map/scatter | solution.py:59
  35.3 9.1 %scatter_fusion.2 = bf16[608,5120]{1,0:T(8,128)(2,1)} fusion(bf16[608,5120]{1,0:T(8,128)(2,1)} %scatter_fusion.1, s32[128]{0:T(128)S(1)} %get-tuple-element.27, bf16[128,5120]{1,0:T(8,128)(2,1)S(1)} %copy-done.2), kind=kCustom, calls=%fused_computation.10 | custom fusion | bytes 3932672 | tf_op jit(solution)/shard_map/scatter | solution.py:59
  44.4 9.0 %scatter_fusion.3 = bf16[608,5120]{1,0:T(8,128)(2,1)} fusion(bf16[608,5120]{1,0:T(8,128)(2,1)} %scatter_fusion.2, s32[128]{0:T(128)S(1)} %get-tuple-element.28, bf16[128,5120]{1,0:T(8,128)(2,1)S(1)} %copy-done.2), kind=kCustom, calls=%fused_computation.11 | custom fusion | bytes 3932672 | tf_op jit(solution)/shard_map/scatter | solution.py:59
  53.4 9.0 %scatter_fusion.4 = bf16[608,5120]{1,0:T(8,128)(2,1)} fusion(bf16[608,5120]{1,0:T(8,128)(2,1)} %scatter_fusion.3, s32[128]{0:T(128)S(1)} %get-tuple-element.29, bf16[128,5120]{1,0:T(8,128)(2,1)S(1)} %copy-done.2), kind=kCustom, calls=%fused_computation.12 | custom fusion | bytes 3932672 | tf_op jit(solution)/shard_map/scatter | solution.py:59
  69.6 102.8 %all_to_all.15 = bf16[32,19,5120]{2,1,0:T(8,128)(2,1)} all-to-all(bf16[32,19,5120]{2,1,0:T(8,128)(2,1)} %reshape.54), channel_id=1, replica_groups=mesh['dp'=4,'expert'=32] {'expert'}, dimensions={0} | all-to-all | bytes 12451840 | tf_op jit(solution)/shard_map/all_to_all | solution.py:61
  179.5 9.1 %fusion.4 = f32[608,768]{1,0:T(8,128)S(1)} fusion(bf16[608,5120]{1,0:T(8,128)(2,1)} %reshape.55, bf16[1,5120,768]{2,1,0:T(8,128)(2,1)} %param.14), kind=kOutput, calls=%fused_computation.25 | convolution fusion | flops 4781506560 | bytes 15958016 | tf_op jit(solution)/shard_map/dot_general | solution.py:63
  189.9 10.2 %fusion.6 = bf16[608,5120]{1,0:T(8,128)(2,1)} fusion(bf16[1,768,5120]{2,1,0:T(8,128)(2,1)} %param.15, f32[608,768]{1,0:T(8,128)S(1)} %fusion.4), kind=kOutput, calls=%fused_computation.27 | convolution fusion | flops 4786954240 | bytes 15958016 | tf_op jit(solution)/shard_map/dot_general | solution.py:65
  220.6 93.5 %all-to-all-done.1 = bf16[32,19,5120]{2,1,0:T(8,128)(2,1)} async-done(((bf16[32,19,5120]{2,1,0:T(8,128)(2,1)}), bf16[32,19,5120]{2,1,0:T(8,128)(2,1)}, u32[]{:S(2)}, u32[]{:S(2)}) %all-to-all-start.1) | async-done | bytes 6225952 | tf_op jit(solution)/shard_map/all_to_all | solution.py:68
  314.1 7.6 reshape.58
  349.5 7.5 gather_fusion.2
  377.1 86.5 %all-gather = f32[163840]{0:T(1024)S(1)} all-gather(f32[5120]{0:T(1024)S(1)} %get-tuple-element.15), channel_id=2, replica_groups=mesh['dp'=4,'expert'=32] {'expert'}, dimensions={0}, use_global_device_ids=true | all-gather | bytes 675840 | tf_op jit(solution)/shard_map/all_gather | solution.py:88
  465.0 80.3 %psum.7 = f32[]{:T(128)} all-reduce(f32[]{:T(128)} %bitcast.23), channel_id=1, replica_groups=mesh['dp'=4,'expert'=32] {'dp','expert'}, use_global_device_ids=true, to_apply=%region_14.15 | all-reduce | flops 1 | bytes 8 | tf_op jit(solution)/shard_map/psum | solution.py:90
  553.7 9.5 %scatter_custom_fusion.7 = bf16[608,5120]{1,0:T(8,128)(2,1)} fusion(bf16[608,5120]{1,0:T(8,128)(2,1)} %scatter_custom_fusion.6, s32[128]{0:T(128)S(1)} %get-tuple-element.25, bf16[128,5120]{1,0:T(8,128)(2,1)S(1)} %copy-done.3, f32[]{:T(128)} %bitcast.25, f32[128]{0:T(128)S(1)} %get-tuple-element.22), kind=kCustom, calls=%fused_computation.55 | custom fusion | flops 2621440 | bytes 7537664 | tf_op jit(solution)/shard_map/scatter | solution.py:99
  563.2 9.1 %scatter_custom_fusion.8 = bf16[608,5120]{1,0:T(8,128)(2,1)} fusion(bf16[608,5120]{1,0:T(8,128)(2,1)} %scatter_custom_fusion.7, s32[128]{0:T(128)S(1)} %get-tuple-element.26, bf16[128,5120]{1,0:T(8,128)(2,1)S(1)} %copy-done.3, f32[]{:T(128)} %bitcast.25, f32[128]{0:T(128)S(1)} %get-tuple-element.21), kind=kCustom, calls=%fused_computation.54 | custom fusion | flops 2621440 | bytes 7537664 | tf_op jit(solution)/shard_map/scatter | solution.py:99
  572.4 9.3 %scatter_custom_fusion.9 = bf16[608,5120]{1,0:T(8,128)(2,1)} fusion(bf16[608,5120]{1,0:T(8,128)(2,1)} %scatter_custom_fusion.8, s32[128]{0:T(128)S(1)} %get-tuple-element.27, bf16[128,5120]{1,0:T(8,128)(2,1)S(1)} %copy-done.3, f32[]{:T(128)} %bitcast.25, f32[128]{0:T(128)S(1)} %get-tuple-element.20), kind=kCustom, calls=%fused_computation.53 | custom fusion | flops 2621440 | bytes 7537664 | tf_op jit(solution)/shard_map/scatter | solution.py:99
  581.7 9.1 %scatter_custom_fusion.10 = bf16[608,5120]{1,0:T(8,128)(2,1)} fusion(bf16[608,5120]{1,0:T(8,128)(2,1)} %scatter_custom_fusion.9, s32[128]{0:T(128)S(1)} %get-tuple-element.28, bf16[128,5120]{1,0:T(8,128)(2,1)S(1)} %copy-done.3, f32[]{:T(128)} %bitcast.25, f32[128]{0:T(128)S(1)} %get-tuple-element.19), kind=kCustom, calls=%fused_computation.52 | custom fusion | flops 2621440 | bytes 7537664 | tf_op jit(solution)/shard_map/scatter | solution.py:99
  590.8 9.1 %scatter_custom_fusion.11 = bf16[608,5120]{1,0:T(8,128)(2,1)} fusion(bf16[608,5120]{1,0:T(8,128)(2,1)} %scatter_custom_fusion.10, s32[128]{0:T(128)S(1)} %get-tuple-element.29, bf16[128,5120]{1,0:T(8,128)(2,1)S(1)} %copy-done.3, f32[]{:T(128)} %bitcast.25, f32[128]{0:T(128)S(1)} %get-tuple-element.18), kind=kCustom, calls=%fused_computation.51 | custom fusion | flops 2621440 | bytes 7537664 | tf_op jit(solution)/shard_map/scatter | solution.py:99
  607.1 96.2 %all_to_all.16 = bf16[32,19,5120]{2,1,0:T(8,128)(2,1)} all-to-all(bf16[32,19,5120]{2,1,0:T(8,128)(2,1)} %reshape.59), channel_id=1, replica_groups=mesh['dp'=4,'expert'=32] {'expert'}, dimensions={0} | all-to-all | bytes 12451840 | tf_op jit(solution)/shard_map/all_to_all | solution.py:102
  710.6 9.6 %multiply_convert_fusion = bf16[608,768]{1,0:T(8,128)(2,1)S(1)} fusion(f32[608,768]{1,0:T(8,128)S(1)} %copy-done.8, bf16[608,5120]{1,0:T(8,128)(2,1)} %reshape.60, bf16[1,768,5120]{2,1,0:T(8,128)(2,1)} %param.15), kind=kOutput, calls=%fused_computation.48 | convolution fusion | flops 4785709056 | bytes 16891904 | tf_op jit(solution)/shard_map/dot_general | solution.py:110
  720.2 11.3 %convolution_convert_fusion.1 = bf16[5120,768]{1,0:T(8,128)(2,1)} fusion(bf16[608,5120]{1,0:T(8,128)(2,1)} %reshape.55, bf16[608,768]{1,0:T(8,128)(2,1)S(1)} %multiply_convert_fusion), kind=kOutput, calls=%fused_computation.20 | convolution fusion | flops 4785438720 | bytes 15024128 | tf_op jit(solution)/shard_map/dot_general | solution.py:17
  731.6 11.4 %convolution_convert_fusion = bf16[768,5120]{1,0:T(8,128)(2,1)} fusion(bf16[608,5120]{1,0:T(8,128)(2,1)} %reshape.60, f32[608,768]{1,0:T(8,128)S(1)} %copy-done.8), kind=kOutput, calls=%fused_computation.19 | convolution fusion | flops 4787773440 | bytes 15958016 | tf_op jit(solution)/shard_map/dot_general | solution.py:17
  743.0 61.1 %reduce-scatter.3.cloned.1.call-done = bf16[1280,768]{1,0:T(8,128)(2,1)} async-done(((bf16[5120,768]{1,0:T(8,128)(2,1)}), bf16[1280,768]{1,0:T(8,128)(2,1)}) %reduce-scatter.3.cloned.1.call-update) | async-done | bytes 1966096 | tf_op jit(solution)/shard_map/reduce_scatter | solution.py:117
  804.2 79.3 %reduce-scatter.5.cloned.1.call-done = bf16[768,1280]{1,0:T(8,128)(2,1)} async-done(((bf16[768,5120]{1,0:T(8,128)(2,1)}), bf16[768,1280]{1,0:T(8,128)(2,1)}) %reduce-scatter.5.cloned.1.call-update) | async-done | bytes 1966096 | tf_op jit(solution)/shard_map/reduce_scatter | solution.py:120
  (61 shorter events, 113.7 us)
Async XLA Ops:
  7.2 206.1 %copy-start = (bf16[5120,160]{0,1:T(8,128)(2,1)S(1)}, bf16[5120,160]{0,1:T(8,128)(2,1)}, u32[]{:S(2)}) copy-start(bf16[5120,160]{0,1:T(8,128)(2,1)} %param.12) | copy-start | bytes 4915204
  9.8 7.0 copy-start.2
  188.7 1.2 copy-start.7
  207.2 5.8 copy-start.4
  207.2 106.9 %all-to-all-start.1 = ((bf16[32,19,5120]{2,1,0:T(8,128)(2,1)}), bf16[32,19,5120]{2,1,0:T(8,128)(2,1)}, u32[]{:S(2)}, u32[]{:S(2)}) async-start(bf16[32,19,5120]{2,1,0:T(8,128)(2,1)} %reshape.57), calls=%async_computation.1 | async-start | bytes 15728640 | tf_op jit(solution)/shard_map/all_to_all | solution.py:68
  212.3 591.9 %reduce-scatter.3.cloned.1.call-start = ((), (), s32[]{:S(2)}) async-start(), calls=%async_computation.5 | async-start | bytes 9830400 | tf_op jit(solution)/shard_map/reduce_scatter | solution.py:117
  364.3 7.4 copy-start.3
  371.7 92.0 %copy-start.5 = (bf16[1,5120]{1,0:T(2,128)(2,1)S(1)}, bf16[1,5120]{1,0:T(2,128)(2,1)}, u32[]{:S(2)}) copy-start(bf16[1,5120]{1,0:T(2,128)(2,1)} %param.19) | copy-start | bytes 30724
  371.7 173.6 %copy-start.6 = (f32[128]{0:T(128)S(1)}, f32[128]{0:T(128)}, u32[]{:S(2)}) copy-start(f32[128]{0:T(128)} %param.17) | copy-start | bytes 1540
  703.3 7.2 copy-start.8
  731.6 151.9 %reduce-scatter.5.cloned.1.call-start = ((), (), s32[]{:S(2)}) async-start(), calls=%async_computation.6 | async-start | bytes 9830400 | tf_op jit(solution)/shard_map/reduce_scatter | solution.py:120
  743.0 140.5 %copy-start.1 = (bf16[5120,160]{0,1:T(8,128)(2,1)S(1)}, bf16[5120,160]{0,1:T(8,128)(2,1)}, u32[]{:S(2)}) copy-start(bf16[5120,160]{0,1:T(8,128)(2,1)} %param.12) | copy-start | bytes 4915204
Sparse Core Ops, SparseCore 0:
  731.7 72.4 reduce-scatter.2
  807.1 76.2 reduce-scatter.4
where the time goes:
time: 902 us; the launch traced here: 893 us
  blocking collectives  366 us (41%)
  waiting for transfers between devices  234 us (26%)
  local copies, waits for them, and re-layouts  153 us (17%)
  other arithmetic  61.8 us (7%)
  matrix products  52.3 us (6%)
  between operations  20.8 us (2%)
    all_to_all x1, blocking collectives, local(): lax.all_to_all(outgoing, 'expert', split_axis=0, concat_axis=0, tiled=True)  103 us
    all_to_all x1, blocking collectives, local(): lax.all_to_all(grad_slots.reshape(experts, capacity, model_width), 'exper...  96.2 us
    all_to_all x1, waiting for transfers between devices, local(): lax.all_to_all(expert_out.reshape(experts, capacity, model_width), 'exper...  93.5 us
    all_gather x1, blocking collectives, local(): group_sums = lax.all_gather(seq_sums, 'expert', axis=0, tiled=True)  86.5 us
    psum x1, blocking collectives, local(): kl_total = lax.psum(jnp.sum(kl_terms), ('dp', 'expert'))  80.3 us
    reduce_scatter x1, waiting for transfers between devices, local(): lax.psum_scatter(down_part.astype(jnp.bfloat16), 'dp', scatter_dimension=...  79.3 us
    reduce_scatter x1, waiting for transfers between devices, local(): lax.psum_scatter(up_part.astype(jnp.bfloat16), 'dp', scatter_dimension=0,...  61.1 us
    scatter x6, other arithmetic, local(): grad_slots.at[slot_index[:, column]]  52.6 us
  transfers between devices with their start and end apart: 3, of which 3 were waited for; matrix products, arithmetic and copies ran while one was open for 2% of the time, Pallas kernels for 0%

commit v1 on v0

v1 whole, which is shorter than its diff:
```python
import jax
import jax.numpy as jnp
from jax import lax
from jax.sharding import PartitionSpec as P

routed_scale = 16.0
kto_beta = 0.1
loss_scale = 1024.0
LANES = 128


def split3(value):
    high = value.astype(jnp.bfloat16)
    rest = value - high.astype(jnp.float32)
    middle = rest.astype(jnp.bfloat16)
    low = (rest - middle.astype(jnp.float32)).astype(jnp.bfloat16)
    return high, middle, low


def contract_rows(left, right):
    return lax.dot_general(
        left, right, (((0,), (0,)), ((), ())), preferred_element_type=jnp.float32
    )


def local(
    tokens,
    router,
    expert_ids,
    w_up,
    w_down,
    readout,
    ref_logp,
    labels,
    prompt_read,
    kl_pair,
    kl_ref,
):
    f32, bf16 = jnp.float32, jnp.bfloat16
    experts = lax.axis_size("expert")
    replicas = lax.axis_size("dp")
    group = lax.axis_index("dp")
    me = lax.axis_index("expert")
    tok_rows, width = tokens.shape
    top_count = expert_ids.shape[1]
    capacity = 4 * tok_rows * top_count // (5 * experts)
    up_matrix = w_up[0]
    down_matrix = w_down[0]
    share = width // experts
    rows = capacity + 1

    logits = jnp.dot(tokens, router, preferred_element_type=f32)
    scores = jnp.exp(logits)
    probs = scores / jnp.sum(scores, axis=1, keepdims=True)
    gates = routed_scale * probs[:, :experts]

    named = jnp.any(
        expert_ids[:, :, None] == jnp.arange(experts, dtype=jnp.int32)[None, None, :], axis=1
    )
    named_f = named.astype(f32)
    tri = (jnp.arange(tok_rows)[:, None] > jnp.arange(tok_rows)[None, :]).astype(bf16)
    rank = jnp.dot(tri, named_f.astype(bf16), preferred_element_type=f32).astype(jnp.int32)
    place = jnp.where(named & (rank < capacity), rank, rows)
    pick = (place.T[:, None, :] == jnp.arange(rows, dtype=jnp.int32)[None, :, None])
    slot_gate = jnp.sum(jnp.where(pick, gates.T[:, None, :], 0.0), axis=2)
    pick = pick.astype(bf16)

    tokens_f = tokens.astype(f32)
    readout_f = readout.astype(f32)
    own_margin = jnp.sum(tokens_f * readout_f) - jnp.sum(ref_logp)
    base = jnp.sum(tokens_f, axis=0).reshape(experts, share)

    sent_x = lax.dot_general(pick, tokens, (((2,), (0,)), ((), ())), preferred_element_type=f32).astype(bf16)
    sent_y = lax.dot_general(pick, readout, (((2,), (0,)), ((), ())), preferred_element_type=f32).astype(bf16)
    last = jnp.concatenate(split3(base) + (jnp.zeros((experts, width - 3 * share), bf16),), axis=1)
    is_last = (jnp.arange(rows) == capacity)[None, :, None]
    sent_x = jnp.where(is_last, last[:, None, :], sent_x)
    sent_y = jnp.where(is_last, prompt_read[0][None, None, :], sent_y)
    pair_column = jnp.where(is_last[:, :, 0], kl_pair[0].astype(f32), slot_gate)
    extra = jnp.stack(split3(pair_column), axis=2)
    extra = jnp.pad(extra, ((0, 0), (0, 0), (0, LANES - 3)))
    sent = jnp.concatenate([sent_x, sent_y, extra], axis=2)
    got = lax.all_to_all(sent, "expert", split_axis=0, concat_axis=0, tiled=True)

    got_gate = jnp.sum(got[:, :, 2 * width : 2 * width + 3].astype(f32), axis=2)
    pair_of = got_gate[:, capacity].astype(jnp.int32)
    gate = jnp.where(jnp.arange(rows)[None, :] == capacity, 0.0, got_gate).reshape(-1, 1)
    x = got[:, :, :width].reshape(experts * rows, width)
    y = got[:, :, width : 2 * width].reshape(experts * rows, width)
    pre_act = jnp.dot(x, up_matrix, preferred_element_type=f32)
    back = lax.dot_general(y, down_matrix, (((1,), (1,)), ((), ())), preferred_element_type=f32)
    logistic = jax.nn.sigmoid(pre_act)
    hidden = pre_act * logistic
    slope = logistic * (1.0 + pre_act * (1.0 - logistic))
    gated = gate * hidden
    margin_part = jnp.sum((gated * back).reshape(experts, -1), axis=1)
    hidden_sum = jnp.sum(gated.reshape(experts, rows, -1), axis=1)
    prompt_down = back.reshape(experts, rows, -1)[:, capacity]
    base_part = jnp.sum(got[:, capacity, : 3 * share].astype(f32).reshape(experts, 3, share), axis=1)
    prompt_part = lax.dynamic_slice_in_dim(got[:, capacity, width : 2 * width], me * share, share, 1).astype(f32)
    pair_hot = (pair_of[:, None] == jnp.arange(experts)[None, :]).astype(f32)
    kl_matrix = lax.dot_general(
        jnp.concatenate([prompt_down, prompt_part], axis=1),
        jnp.concatenate([hidden_sum, base_part], axis=1),
        (((1,), (1,)), ((), ())),
        precision=lax.Precision.HIGHEST,
        preferred_element_type=f32,
    )
    kl_part = jnp.sum(kl_matrix * pair_hot, axis=1)
    own = jnp.arange(experts) == me
    margin_part = margin_part + jnp.where(own, own_margin, 0.0)
    kl_part = kl_part - jnp.where(own, kl_ref[0], 0.0)
    label_part = jnp.where(own, jnp.where(labels[0] == 1, 1.0, -1.0), 0.0)
    mine = jnp.stack([margin_part, kl_part, label_part])
    spread = jnp.where(jnp.arange(replicas)[:, None, None] == group, mine[None], 0.0)
    total = lax.psum(spread.reshape(-1), ("dp", "expert")).reshape(replicas, 3, experts)
    anchor = jnp.sum(total[:, 1]) / (experts * replicas)
    here = lax.dynamic_index_in_dim(total, group, 0, keepdims=False)
    margins, kl_all, signed = here[0], here[1], here[2]
    kept = jax.nn.sigmoid(kto_beta * signed * (margins - anchor))
    margin_grad = -loss_scale * kto_beta * signed * kept * (1.0 - kept)
    losses = lax.dynamic_slice_in_dim(1.0 - kept, me, 1)
    kl_terms = lax.dynamic_slice_in_dim(kl_all, me, 1)

    row_grad = jnp.broadcast_to(margin_grad[:, None], (experts, rows)).reshape(-1, 1)
    pre_grad = (gate * row_grad * back * slope).astype(bf16)
    scaled = (gated * row_grad).astype(bf16)
    up_part = contract_rows(x, pre_grad).astype(bf16)
    down_part = contract_rows(scaled, y).astype(bf16)
    grad_up = lax.psum_scatter(up_part, "dp", scatter_dimension=0, tiled=True)[None]
    grad_down = lax.psum_scatter(down_part, "dp", scatter_dimension=1, tiled=True)[None]
    return (grad_up, grad_down, losses, kl_terms)


def solution(mesh):
    return jax.shard_map(
        local,
        mesh=mesh,
        in_specs=(
            P(("dp", "expert"), None),
            P(),
            P(("dp", "expert"), None),
            P("expert", None, None),
            P("expert", None, None),
            P(("dp", "expert"), None),
            P(("dp", "expert")),
            P(("dp", "expert")),
            P(("dp", "expert"), None),
            P(("dp", "expert")),
            P(("dp", "expert")),
        ),
        out_specs=(
            P("expert", "dp", None),
            P("expert", None, "dp"),
            P(("dp", "expert")),
            P(("dp", "expert")),
        ),
        check_vma=False,
    )
```

time: 902 us -> 624 us (0.69)
  blocking collectives: 366 us -> 90.2 us
  waiting for transfers between devices: 234 us -> 376 us
  local copies, waits for them, and re-layouts: 153 us -> 52.5 us
  other arithmetic: 61.8 us -> 18.8 us
    all_to_all x2 -> x0, blocking collectives: 199 us -> none  [the longest x1 103 us: local(): lax.all_to_all(outgoing, 'expert', split_axis=0, concat_axis=0, tiled=True)]
    all_to_all x1, waiting for transfers between devices: 93.5 us -> 237 us  [local(): lax.all_to_all(sent, 'expert', split_axis=0, concat_axis=0, tiled=True)]
    all_gather x1 -> x0, blocking collectives: 86.5 us -> none  [local(): group_sums = lax.all_gather(seq_sums, 'expert', axis=0, tiled=True)]
    scatter x6 -> x0, other arithmetic: 52.6 us -> none  [local(): grad_slots.at[slot_index[:, column]]]
    scatter x6 -> x0, local copies, waits for them, and re-layouts: 52.6 us -> none  [local(): outgoing = outgoing.at[slot_index[:, column]].set(tokens, mode='drop')]
    gather x11 -> x0, local copies, waits for them, and re-layouts: 49.6 us -> none  [the longest x6 44.1 us: local(): returned_rows[slot_index[:, column]].astype(jnp.float32)]
    reshape x6, local copies, waits for them, and re-layouts: 43.3 us -> 23 us  [the longest x1 8.7 us: local(): x = got[:, :, :width].reshape(experts * rows, width)]
    slice x0 -> x3, local copies, waits for them, and re-layouts: none -> 14.6 us  [the longest x1 10.9 us: local(): y = got[:, :, width:2 * width].reshape(experts * rows, width)]
where the time goes in v1:
time: 624 us; the launch traced here: 623 us
  waiting for transfers between devices  376 us (60%)
  blocking collectives  90.2 us (14%)
  matrix products  55.7 us (9%)
  local copies, waits for them, and re-layouts  52.5 us (8%)
  other arithmetic  18.8 us (3%)
  between operations  18.4 us (3%)
  starting transfers between devices  11.9 us (2%)
    all_to_all x1, waiting for transfers between devices, local(): lax.all_to_all(sent, 'expert', split_axis=0, concat_axis=0, tiled=True)  237 us
    psum x1, blocking collectives, local(): lax.psum(spread.reshape(-1), ('dp', 'expert')).reshape(replicas, 3, experts)  90.2 us
    reduce_scatter x1, waiting for transfers between devices, local(): lax.psum_scatter(down_part, 'dp', scatter_dimension=1, tiled=True)[None]  79.3 us
    reduce_scatter x1, waiting for transfers between devices, local(): lax.psum_scatter(up_part, 'dp', scatter_dimension=0, tiled=True)[None]  59.7 us
    dot_general x2, matrix products, contract_rows(): lax.dot_general(left, right, (((0,), (0,)), ((), ())), preferred_element_...  24.1 us
    dot_general x1, matrix products, local(): lax.dot_general(y, down_matrix, (((1,), (1,)), ((), ())), preferred_eleme...  13.2 us
  transfers between devices with their start and end apart: 3, of which 3 were waited for; matrix products, arithmetic and copies ran while one was open for 2% of the time, Pallas kernels for 0%

profile of v1, /device:TPU:1, one launch (start us, length us, event | category | flops | bytes accessed | tf_op | source)
XLA Modules:
  0.0 623.2 jit_solution(5066378611286889165)
XLA Ops:
  8.9 1.9 fusion.35
  11.2 3.1 fusion.6
  15.0 4.6 broadcast_select_fusion.1
  19.7 1.8 broadcast_select_fusion
  22.6 8.6 %fusion.1 = bf16[32,20,10368]{2,0,1:T(8,128)(2,1)S(1)} fusion(bf16[32,20,3]{2,0,1:T(8,128)(2,1)S(1)} %copy.34, bf16[32,20,5120]{2,0,1:T(8,128)(2,1)S(1)} %broadcast_select_fusion, bf16[32,20,5120]{2,0,1:T(8,128)(2,1)S(1)} %copy-done.2), kind=kLoop, calls=%fused_computation.2 | loop fusion | flops 53084160 | bytes 26382080 | tf_op jit(solution)/shard_map/concatenate | solution.py:82
  31.2 11.6 %copy.35 = bf16[32,20,10368]{2,1,0:T(8,128)(2,1)} copy(bf16[32,20,10368]{2,0,1:T(8,128)(2,1)S(1)} %fusion.1) | data formatting | bytes 26542080 | tf_op jit(solution)/shard_map/concatenate | solution.py:82
  42.7 11.6 %all-to-all-start = ((bf16[32,20,10368]{2,1,0:T(8,128)(2,1)}), bf16[32,20,10368]{2,1,0:T(8,128)(2,1)}, u32[]{:S(2)}, u32[]{:S(2)}) async-start(bf16[32,20,10368]{2,1,0:T(8,128)(2,1)} %copy.35), calls=%async_computation | async-start | bytes 31850496 | tf_op jit(solution)/shard_map/all_to_all | solution.py:83
  57.8 236.8 %all-to-all-done = bf16[32,20,10368]{2,1,0:T(8,128)(2,1)} async-done(((bf16[32,20,10368]{2,1,0:T(8,128)(2,1)}), bf16[32,20,10368]{2,1,0:T(8,128)(2,1)}, u32[]{:S(2)}, u32[]{:S(2)}) %all-to-all-start) | async-done | bytes 13271072 | tf_op jit(solution)/shard_map/all_to_all | solution.py:83
  296.0 1.2 fusion.22
  297.4 10.9 %fusion.34 = (bf16[32,20,5120]{2,1,0:T(8,128)(2,1)}, bf16[32,20,5120]{2,1,0:T(8,128)(2,1)}) fusion(bf16[32,20,10368]{2,1,0:T(8,128)(2,1)} %all-to-all-done), kind=kLoop, calls=%fused_computation.86 | loop fusion | bytes 26214400 | tf_op jit(solution)/shard_map/slice | solution.py:89
  308.4 8.7 %reshape.267 = bf16[640,5120]{1,0:T(8,128)(2,1)} reshape(bf16[32,20,5120]{2,1,0:T(8,128)(2,1)} %get-tuple-element.10) | data formatting | bytes 13107200 | tf_op jit(solution)/shard_map/reshape | solution.py:89
  317.0 2.4 slice.57
  319.6 8.7 %reshape.266 = bf16[640,5120]{1,0:T(8,128)(2,1)} reshape(bf16[32,20,5120]{2,1,0:T(8,128)(2,1)} %get-tuple-element.11) | data formatting | bytes 13107200 | tf_op jit(solution)/shard_map/reshape | solution.py:88
  328.3 9.7 %fusion.4 = f32[640,768]{1,0:T(8,128)S(1)} fusion(bf16[640,5120]{1,0:T(8,128)(2,1)} %reshape.266, bf16[1,5120,768]{2,1,0:T(8,128)(2,1)} %param.14), kind=kOutput, calls=%fused_computation.9 | convolution fusion | flops 5033164800 | bytes 16384000 | tf_op jit(solution)/shard_map/dot_general | solution.py:90
  338.0 13.2 %multiply_reduce_fusion = (f32[640]{0:T(1024)S(1)}, f32[640,768]{1,0:T(8,128)}, f32[640,768]{1,0:T(8,128)}) fusion(f32[640,768]{1,0:T(8,128)S(1)} %fusion.4, f32[640]{0:T(1024)S(1)} %select_n.115, bf16[640,5120]{1,0:T(8,128)(2,1)} %reshape.267, bf16[1,768,5120]{2,1,0:T(8,128)(2,1)} %param.15), kind=kOutput, calls=%fused_computation.18 | convolution fusion | flops 5036604928 | bytes 20321280 | tf_op jit(solution)/shard_map/dot_general | solution.py:91
  351.3 2.7 reshape.269
  354.1 2.0 reduce_sum.123
  356.1 2.7 reshape.268
  358.8 1.2 slice.56
  360.4 90.2 %psum.7 = f32[4,3,32]{2,1,0:T(4,128)S(1)} all-reduce(f32[4,3,32]{2,1,0:T(4,128)S(1)} %broadcast_select_fusion.3), channel_id=1, replica_groups=mesh['dp'=4,'expert'=32] {'dp','expert'}, use_global_device_ids=true, to_apply=%region_12.13 | all-reduce | flops 384 | bytes 3072 | tf_op jit(solution)/shard_map/psum | solution.py:116
  452.0 12.1 %convolution_convert_fusion = bf16[5120,768]{1,0:T(8,128)(2,1)} fusion(bf16[640,5120]{1,0:T(8,128)(2,1)} %reshape.266, f32[640,768]{1,0:T(8,128)} %copy-done.7, f32[640,768]{1,0:T(8,128)} %get-tuple-element.20, f32[640]{0:T(1024)S(1)} %mul.125), kind=kOutput, calls=%fused_computation.3 | convolution fusion | flops 5042012160 | bytes 18352640 | tf_op jit(solution)/shard_map/dot_general | solution.py:21
  464.2 12.0 %convolution_convert_fusion.1 = bf16[768,5120]{1,0:T(8,128)(2,1)} fusion(bf16[640,5120]{1,0:T(8,128)(2,1)} %reshape.267, f32[640,768]{1,0:T(8,128)} %get-tuple-element.9, f32[640]{0:T(1024)S(1)} %reshape.271), kind=kOutput, calls=%fused_computation.4 | convolution fusion | flops 5038080000 | bytes 16386560 | tf_op jit(solution)/shard_map/dot_general | solution.py:21
  477.4 59.7 %reduce-scatter.3.cloned.1.call-done = bf16[1280,768]{1,0:T(8,128)(2,1)} async-done(((bf16[5120,768]{1,0:T(8,128)(2,1)}), bf16[1280,768]{1,0:T(8,128)(2,1)}) %reduce-scatter.3.cloned.1.call-update) | async-done | bytes 1966096 | tf_op jit(solution)/shard_map/reduce_scatter | solution.py:130
  537.1 79.3 %reduce-scatter.5.cloned.1.call-done = bf16[768,1280]{1,0:T(8,128)(2,1)} async-done(((bf16[768,5120]{1,0:T(8,128)(2,1)}), bf16[768,1280]{1,0:T(8,128)(2,1)}) %reduce-scatter.5.cloned.1.call-update) | async-done | bytes 1966096 | tf_op jit(solution)/shard_map/reduce_scatter | solution.py:131
  (61 shorter events, 8.2 us)
Async XLA Ops:
  7.2 1.8 copy-start
  7.2 7.9 %copy-start.3 = (bf16[128,5120]{1,0:T(8,128)(2,1)S(1)}, bf16[128,5120]{1,0:T(8,128)(2,1)}, u32[]{:S(2)}) copy-start(bf16[128,5120]{1,0:T(8,128)(2,1)} %param.11) | copy-start | bytes 3932164
  10.9 8.8 %copy-start.5 = (bf16[1,5120]{1,0:T(2,128)(2,1)S(1)}, bf16[1,5120]{1,0:T(2,128)(2,1)}, u32[]{:S(2)}) copy-start(bf16[1,5120]{1,0:T(2,128)(2,1)} %param.19) | copy-start | bytes 30724
  10.9 8.8 %copy-start.4 = (bf16[128,5120]{1,0:T(8,128)(2,1)S(1)}, bf16[128,5120]{1,0:T(8,128)(2,1)}, u32[]{:S(2)}) copy-start(bf16[128,5120]{1,0:T(8,128)(2,1)} %param.16) | copy-start | bytes 3932164
  19.7 2.9 copy-start.2
  42.7 13.1 %copy-start.6 = (f32[128]{0:T(128)S(1)}, f32[128]{0:T(128)}, u32[]{:S(2)}) copy-start(f32[128]{0:T(128)} %param.17) | copy-start | bytes 1540
  42.7 251.9 %all-to-all-start = ((bf16[32,20,10368]{2,1,0:T(8,128)(2,1)}), bf16[32,20,10368]{2,1,0:T(8,128)(2,1)}, u32[]{:S(2)}, u32[]{:S(2)}) async-start(bf16[32,20,10368]{2,1,0:T(8,128)(2,1)} %copy.35), calls=%async_computation | async-start | bytes 31850496 | tf_op jit(solution)/shard_map/all_to_all | solution.py:83
  54.3 482.7 %reduce-scatter.3.cloned.1.call-start = ((), (), s32[]{:S(2)}) async-start(), calls=%async_computation.3 | async-start | bytes 9830400 | tf_op jit(solution)/shard_map/reduce_scatter | solution.py:130
  337.9 13.2 %copy-start.7 = (f32[640,768]{1,0:T(8,128)}, f32[640,768]{1,0:T(8,128)S(1)}, u32[]{:S(2)}) copy-start(f32[640,768]{1,0:T(8,128)S(1)} %fusion.4) | copy-start | bytes 5898244
  464.1 152.2 %reduce-scatter.5.cloned.1.call-start = ((), (), s32[]{:S(2)}) async-start(), calls=%async_computation.4 | async-start | bytes 9830400 | tf_op jit(solution)/shard_map/reduce_scatter | solution.py:131
  464.2 152.2 %copy-start.1 = (bf16[5120,160]{0,1:T(8,128)(2,1)S(1)}, bf16[5120,160]{0,1:T(8,128)(2,1)}, u32[]{:S(2)}) copy-start(bf16[5120,160]{0,1:T(8,128)(2,1)} %param.12) | copy-start | bytes 4915204
Sparse Core Ops, SparseCore 0:
  464.3 72.7 reduce-scatter.2
  540.1 76.2 reduce-scatter.4

commit v2 on v1

v2 whole, which is shorter than its diff:
```python
import functools

import jax
import jax.numpy as jnp
from jax import lax
from jax.experimental import pallas as pl
from jax.experimental.pallas import tpu as pltpu
from jax.sharding import PartitionSpec as P

MESH = pl.DeviceIdType.MESH
routed_scale = 16.0
kto_beta = 0.1
loss_scale = 1024.0
f32, bf16 = jnp.float32, jnp.bfloat16

RING = 4
COLUMNS = 16
LANES = 128
META = 80
NT = (((1,), (1,)), ((), ()))
TN = (((0,), (0,)), ((), ()))


def split3(value):
    high = value.astype(bf16).astype(f32)
    middle = (value - high).astype(bf16).astype(f32)
    low = (value - high - middle).astype(bf16).astype(f32)
    return high, middle, low


def place():
    dp, ex = lax.axis_index("dp"), lax.axis_index("expert")
    return dp // 2, dp % 2, ex % 2, ex // 2


def kernel(
    cap, hw, tok, rdo, meta, own, wu_hbm, wd_hbm,
    up_out, down_out, small_out,
    xb, yb, mb, ob, xin, yin, wu, wd, pa, ra, pas, pap, ras, rap, prs, hst, wst,
    exty, hst_t, gsd, grd, acc, arb, arc,
    lsem, ag_s, ag_r, xs, xr, ys, yr, ps, pr, qs, qr, ar_s, ar_r, c_s, c_r, g_s, g_r,
):
    rb = META
    tr = tok.shape[0]
    hid = wu.shape[1]
    x_lo, core, x_hi, col = place()
    dp, ex = lax.axis_index("dp"), lax.axis_index("expert")
    x = x_hi * 2 + x_lo
    y, z = col % RING, col // RING

    def dev_x(xx):
        return ((xx % 2) * 2 + core, col * 2 + xx // 2)

    def dev_col(cc):
        return (dp, cc * 2 + x_hi)

    sibling = (x_lo * 2 + 1 - core, ex)
    partner = ((1 - x_lo) * 2 + core, ex)

    def column_at(k):
        return ((z + k // RING) % RING) * RING + (y + k % RING) % RING

    def column_from(k):
        return ((z + RING - k // RING) % RING) * RING + (y + RING - k % RING) % RING

    def rows_of(cc):
        return pl.ds(pl.multiple_of(cc * rb, 16), rb)

    def tail_of(cc):
        return pl.ds(pl.multiple_of(cc * rb + 64, 16), 16)

    def remote(src, dst, ss, rs, dev):
        return pltpu.make_async_remote_copy(
            src_ref=src, dst_ref=dst, send_sem=ss, recv_sem=rs, device_id=dev, device_id_type=MESH
        )

    barrier = pltpu.get_barrier_semaphore()
    for d in range(1, RING):
        pl.semaphore_signal(barrier, inc=1, device_id=dev_x((x + d) % RING), device_id_type=MESH)

    def greet(k, carry):
        pl.semaphore_signal(barrier, inc=1, device_id=dev_col(column_at(k)), device_id_type=MESH)
        return carry

    lax.fori_loop(1, COLUMNS, greet, 0)
    pl.semaphore_signal(barrier, inc=1, device_id=sibling, device_id_type=MESH)
    half = pl.ds(pl.multiple_of(x_lo * hw, LANES), hw)
    mine = pl.ds(pl.multiple_of(x * tr, LANES), tr)
    locals_ = [
        pltpu.make_async_copy(tok.at[:, half], xb.at[mine], lsem.at[0]),
        pltpu.make_async_copy(rdo.at[:, half], yb.at[mine], lsem.at[1]),
        pltpu.make_async_copy(meta.at[x], mb.at[x], lsem.at[2]),
        pltpu.make_async_copy(wu_hbm.at[half], wu, lsem.at[3]),
        pltpu.make_async_copy(wd_hbm.at[:, half], wd.at[pl.ds(0, hid)], lsem.at[4]),
    ]
    for copy in locals_:
        copy.start()
    pl.semaphore_wait(barrier, RING - 1 + COLUMNS - 1 + 1)

    def ring_copy(which, d):
        to = (x + d) % RING
        cols = pl.ds(pl.multiple_of((to % 2) * hw, LANES), hw)
        src = (meta.at[to], tok.at[:, cols], rdo.at[:, cols])[which]
        dst = (mb.at[x], xb.at[mine], yb.at[mine])[which]
        return remote(src, dst, ag_s.at[which * 3 + d - 1], ag_r.at[which * 3 + d - 1], dev_x(to))

    sends = [ring_copy(which, d) for which in (0, 1) for d in (1, 3, 2)]
    for copy in sends:
        copy.start()
    for copy in sends:
        copy.wait_recv()
    later = [ring_copy(2, d) for d in (1, 3, 2)]
    for copy in later:
        copy.start()
    for copy in locals_:
        copy.wait()

    exty[...] = jnp.zeros_like(exty)
    base_rows = [[], []]
    for j in range(hw // LANES):
        lane = pl.ds(j * LANES, LANES)
        for b in range(RING):
            exty[12 + b : 13 + b, lane] = mb[b, 32 + j : 33 + j, :]
    tall = lax.broadcasted_iota(jnp.int32, (LANES, LANES), 0)
    for j in range(hw // LANES):
        lane = pl.ds(j * LANES, LANES)
        terms = split3(mb[x, 52 + j : 53 + j, :]) + split3(mb[x + 1 - 2 * x_lo, 52 + j : 53 + j, :])
        block = jnp.zeros((LANES, LANES), f32)
        for i, term in enumerate(terms):
            block = jnp.where(tall == i, term, block)
        wd[pl.ds(hid, LANES), lane] = block.astype(bf16)

    wide = 512

    def picks(cc):
        want = jnp.concatenate([mb[b, pl.ds(cc, 1), :] for b in range(RING)], axis=1)
        row = lax.broadcasted_iota(jnp.int32, (LANES, RING * tr), 0).astype(f32)
        return jnp.where(row == want, 1.0, 0.0).astype(bf16)

    def x_copy(k):
        to = column_at(k)
        return remote(ob.at[rows_of(to)], xin.at[rows_of(col)], xs.at[k], xr.at[k], dev_col(to))

    def y_copy(k):
        to = column_at(k)
        return remote(ob.at[rows_of(to)], yin.at[rows_of(col)], ys.at[k], yr.at[k], dev_col(to))

    def build(cc, src, dst, extra):
        pick = picks(cc)
        for j in range(hw // wide):
            lane = pl.ds(j * wide, wide)
            block = jnp.dot(pick[:rb], src[:, lane], preferred_element_type=f32)
            dst[rows_of(cc), lane] = block.astype(bf16)
            tail = extra(j, pick, block[64:rb])
            if tail is not None:
                dst[tail_of(cc), lane] = tail.astype(bf16)

    def x_extra(cc):
        def extra(j, pick, tail):
            if j:
                return None
            gate = jnp.concatenate([mb[b, pl.ds(16 + cc, 1), :] for b in range(RING)], axis=1)
            row = lax.broadcasted_iota(jnp.int32, (16, RING * tr), 0)
            lifted = jnp.zeros((16, RING * tr), f32)
            for i, term in enumerate(split3(gate)):
                lifted = jnp.where(row == 12 + i, term, lifted)
            gates = lax.dot_general(lifted.astype(bf16), pick, NT, preferred_element_type=f32)
            pair = [sum(mb[b, 72 + i : 73 + i, :] for b in range(RING)) for i in range(2)]
            pair = jnp.concatenate(pair + [jnp.zeros((1, wide - 2 * LANES), f32)], axis=1)
            last = lax.broadcasted_iota(jnp.int32, (16, wide), 0) == 15
            gates = jnp.concatenate([gates, jnp.zeros((16, wide - LANES), f32)], axis=1)
            return tail + gates + jnp.where(last, pair, 0.0)

        return extra

    def y_extra(j, pick, tail):
        return tail + exty[:, pl.ds(j * wide, wide)]

    def send_x(k, carry):
        to = column_at(k)
        build(to, xb, ob, x_extra(to))
        x_copy(k).start()
        return carry

    lax.fori_loop(1, COLUMNS, send_x, 0)
    build(col, xb, xin, x_extra(col))
    for copy in later:
        copy.wait_recv()

    def send_y(k, carry):
        to = column_at(k)
        x_copy(k).wait_send()
        build(to, yb, ob, y_extra)
        y_copy(k).start()
        return carry

    lax.fori_loop(1, COLUMNS, send_y, 0)
    build(col, yb, yin, y_extra)

    def pair_x(k):
        at = rows_of(column_from(k))
        return remote(pas.at[at], pap.at[at], ps.at[k], pr.at[k], partner)

    def pair_y(k):
        at = rows_of(column_from(k))
        return remote(ras.at[at], rap.at[at], qs.at[k], qr.at[k], partner)

    def use_x(k, carry):
        at = rows_of(column_from(k))

        @pl.when(k > 0)
        def _():
            x_copy(k).wait_recv()

        part = jnp.dot(xin[at, :], wu[...], preferred_element_type=f32)
        pa[at, :] = part
        pas[at, :] = part.astype(bf16)
        pair_x(k).start()
        return carry

    lax.fori_loop(0, COLUMNS, use_x, 0)

    lane256 = lax.broadcasted_iota(jnp.int32, (rb, 2 * LANES), 1)
    row256 = lax.broadcasted_iota(jnp.int32, (rb, 2 * LANES), 0)
    row_lane = jnp.where(row256 < RING * cap, 12 + row256 // cap, -1)

    def block_of(cc):
        return lane256 - cc * 16 == row_lane

    acc[...] = own[...]

    def meet(k):
        cc = column_from(k)
        at = rows_of(cc)
        pair_x(k).wait_recv()
        pair_y(k).wait_recv()
        p = pa[at, :] + pap[at, :].astype(f32)
        r = ra[at, :] + rap[at, :].astype(f32)
        gate = jnp.sum(xin[tail_of(cc), pl.ds(0, LANES)].astype(f32)[12:15], axis=0, keepdims=True)
        square = lax.broadcasted_iota(jnp.int32, (rb, LANES), 0) == lax.broadcasted_iota(
            jnp.int32, (rb, LANES), 1
        )
        gate = jnp.sum(jnp.where(square, gate, 0.0), axis=1, keepdims=True)
        logistic = jax.nn.sigmoid(p)
        gated = gate * (p * logistic)
        prs[pl.ds(pl.multiple_of(cc * 16, 16), 16), :] = r[64:rb]
        pa[at, :] = gated
        ra[at, :] = gate * r * (logistic * (1.0 + p * (1.0 - logistic)))
        margin = jnp.sum(gated * r, axis=1, keepdims=True)
        hot = jnp.where(block_of(cc), 1.0, 0.0)
        acc[1:2, :] += 0.5 * jnp.sum(hot * margin, axis=0, keepdims=True)
        acc[3:4, :] += xin[tail_of(cc), pl.ds(0, 2 * LANES)].astype(f32)[15:16]
        first = lax.broadcasted_iota(jnp.int32, (16, rb), 0)
        which = lax.broadcasted_iota(jnp.int32, (16, rb), 1) // cap
        rows = jnp.where(first == which, 1.0, 0.0).astype(bf16)
        hst[pl.ds(pl.multiple_of(cc * 16, 16), 16), :] = jnp.dot(
            rows, gated.astype(bf16), preferred_element_type=f32
        )

    lag = 2

    def use_y(k, carry):
        cc = column_from(k)
        at = rows_of(cc)

        @pl.when(k > 0)
        def _():
            y_copy(k).wait_recv()

        part = lax.dot_general(yin[at, :], wd[...], NT, preferred_element_type=f32)
        ra[at, :] = part[:, :hid]
        ras[at, :] = part[:, :hid].astype(bf16)
        wst[pl.ds(pl.multiple_of(cc * 16, 16), 16), :] = part[64:rb, hid:]
        pair_y(k).start()

        @pl.when(k >= lag)
        def _():
            meet(k - lag)

        return carry

    lax.fori_loop(0, COLUMNS, use_y, 0)

    def finish(k, carry):
        meet(k)
        return carry

    lax.fori_loop(COLUMNS - lag, COLUMNS, finish, 0)

    def drain(k, carry):
        pair_x(k).wait_send()
        pair_y(k).wait_send()

        @pl.when(k > 0)
        def _():
            y_copy(k).wait_send()

        return carry

    wide_t = wst[...].T
    base_own = wide_t[0:1] + wide_t[1:2] + wide_t[2:3]
    base_other = wide_t[3:4] + wide_t[4:5] + wide_t[5:6]
    pairs = acc[3:4, :]
    terms = 0.5 * lax.dot_general(
        hst[...], prs[...], NT, precision=lax.Precision.HIGHEST, preferred_element_type=f32
    )
    named = lax.broadcasted_iota(jnp.int32, terms.shape, 0)
    terms += jnp.where(named == col * 16 + x, base_own, 0.0)
    terms += jnp.where(named == col * 16 + x + 1 - 2 * x_lo, base_other, 0.0)
    used = lax.broadcasted_iota(jnp.int32, (1, 2 * LANES), 1) % 16 >= 12
    chosen = jnp.where((named.astype(f32) == pairs) & used, terms, 0.0)
    acc[0:1, :] += jnp.sum(chosen, axis=0, keepdims=True)

    def ring_sum(axis, dev):
        copies = [
            remote(acc, arb.at[axis * 3 + d - 1], ar_s.at[axis * 3 + d - 1], ar_r.at[axis * 3 + d - 1], dev(d))
            for d in (1, 3, 2)
        ]
        for copy in copies:
            copy.start()
        for copy in copies:
            copy.wait()
        acc[...] = acc[...] + arb[axis * 3] + arb[axis * 3 + 1] + arb[axis * 3 + 2]

    ring_sum(0, lambda d: dev_x((x + d) % RING))
    ring_sum(1, lambda d: dev_col(z * RING + (y + d) % RING))
    ring_sum(2, lambda d: dev_col(((z + d) % RING) * RING + y))
    lax.fori_loop(0, COLUMNS, drain, 0)
    for copy in sends + later:
        copy.wait_send()
    swap = remote(acc, arc, c_s.at[0], c_r.at[0], sibling)
    swap.start()
    swap.wait()
    kl_row = jnp.where(used, acc[0:1, :], 0.0)
    kl_other = jnp.where(used, arc[0:1, :], 0.0)
    count = RING * COLUMNS * 2
    anchor = jnp.sum(kl_row + kl_other, axis=1, keepdims=True) / count
    signed = acc[2:3, :]
    kept = jax.nn.sigmoid(kto_beta * signed * (acc[1:2, :] - anchor))
    slope = -loss_scale * kto_beta * signed * kept * (1.0 - kept)
    small_out[...] = jnp.zeros_like(small_out)
    small_out[0:1, :] = 1.0 - kept
    small_out[1:2, :] = kl_row

    def scale(cc, carry):
        at = rows_of(cc)
        factor = jnp.sum(jnp.where(block_of(cc), slope, 0.0), axis=1, keepdims=True)
        pas[at, :] = (pa[at, :] * factor).astype(bf16)
        ras[at, :] = (ra[at, :] * factor).astype(bf16)
        return carry

    lax.fori_loop(0, COLUMNS, scale, 0)
    for j in range(5):
        at = pl.ds(j * 256, 256)
        hst_t[:, at] = pas[at, :].T

    quarter = hw // 2
    step = 256
    other = (1 - core) * quarter
    this = core * quarter

    def up_block(start, j):
        at = pl.ds(pl.multiple_of(start + j * step, LANES), step)
        return lax.dot_general(xin[:, at], ras[...], TN, preferred_element_type=f32)

    def down_block(start, j):
        at = pl.ds(pl.multiple_of(start + j * step, LANES), step)
        return jnp.dot(hst_t[...], yin[:, at], preferred_element_type=f32)

    def piece(j):
        return pl.ds(pl.multiple_of(j * step, step), step)

    def other_up(j, carry):
        pap[piece(j), :] = up_block(other, j).astype(bf16)
        return carry

    def other_down(j, carry):
        gsd[:, piece(j)] = down_block(other, j).astype(bf16)
        return carry

    def this_up(j, carry):
        up_out[piece(j), :] = (up_block(this, j) + rap[piece(j), :].astype(f32)).astype(bf16)
        return carry

    def this_down(j, carry):
        down_out[:, piece(j)] = (down_block(this, j) + grd[:, piece(j)].astype(f32)).astype(bf16)
        return carry

    up_copy = remote(pap, rap, g_s.at[0], g_r.at[0], sibling)
    down_copy = remote(gsd, grd, g_s.at[1], g_r.at[1], sibling)
    lax.fori_loop(0, quarter // step, other_up, 0)
    up_copy.start()
    lax.fori_loop(0, quarter // step, other_down, 0)
    down_copy.start()
    up_copy.wait_recv()
    lax.fori_loop(0, quarter // step, this_up, 0)
    down_copy.wait_recv()
    lax.fori_loop(0, quarter // step, this_down, 0)
    up_copy.wait_send()
    down_copy.wait_send()


def local(
    tokens, router, expert_ids, w_up, w_down, readout, ref_logp, labels, prompt_read, kl_pair, kl_ref
):
    experts = lax.axis_size("expert")
    tr, width = tokens.shape
    top = expert_ids.shape[1]
    cap = 4 * tr * top // (5 * experts)
    hid = w_up.shape[2]
    hw = width // 2
    x_lo, core, x_hi, col = place()
    x = x_hi * 2 + x_lo

    logits = jnp.dot(tokens, router, preferred_element_type=f32)
    scores = jnp.exp(logits)
    gates = routed_scale * (scores / jnp.sum(scores, axis=1, keepdims=True))[:, :experts]
    named = jnp.any(expert_ids[:, :, None] == jnp.arange(experts, dtype=jnp.int32), axis=1)
    before = (jnp.arange(tr)[:, None] > jnp.arange(tr)[None, :]).astype(bf16)
    rank = jnp.dot(before, named.astype(bf16), preferred_element_type=f32)
    want = jnp.where(named & (rank < cap), rank + (cap * x).astype(f32), -1.0)
    by_expert = jnp.stack([want, gates]).transpose(2, 0, 1).reshape(COLUMNS, 2, 2, tr)
    by_expert = by_expert.transpose(1, 2, 0, 3).reshape(2, 2 * COLUMNS, tr)

    tokens_f = tokens.astype(f32)
    own_margin = jnp.sum(tokens_f * readout.astype(f32)) - jnp.sum(ref_logp)
    base = jnp.sum(tokens_f, axis=0).reshape(2, hw // LANES, LANES)
    prompt = prompt_read.astype(f32).reshape(2, hw // LANES, LANES)
    lane = jnp.arange(2 * LANES)
    spot = lane == col * 16 + 12 + x
    pair = (kl_pair[0] // 2) * 16 + (kl_pair[0] % 2) * 2 + x_lo
    misc = jnp.pad(jnp.where(spot, pair, 0).astype(f32).reshape(2, LANES), ((0, 6), (0, 0)))
    per_half = jnp.concatenate([prompt, base], axis=1)
    meta = jnp.concatenate(
        [
            jnp.repeat(by_expert, 2, axis=0),
            jnp.concatenate([per_half, per_half], axis=0),
            jnp.broadcast_to(misc, (RING, 8, LANES)),
        ],
        axis=1,
    )
    sign = jnp.where(labels[0] == 1, 1.0, -1.0)
    own = jnp.where(spot[None, :], jnp.stack([-kl_ref[0], own_margin, sign])[:, None], 0.0)
    own = jnp.pad(own, ((0, 5), (0, 0)))

    slots = COLUMNS * META
    quarter = hw // 2
    dma = pltpu.SemaphoreType.DMA
    any_ = pl.BlockSpec(memory_space=pl.ANY)
    vmem = pl.BlockSpec(memory_space=pltpu.VMEM)
    up, down, small = pl.pallas_call(
        functools.partial(kernel, cap, hw),
        out_shape=(
            jax.ShapeDtypeStruct((quarter, hid), bf16),
            jax.ShapeDtypeStruct((hid, quarter), bf16),
            jax.ShapeDtypeStruct((8, 2 * LANES), f32),
        ),
        in_specs=[any_, any_, any_, vmem, any_, any_],
        out_specs=(vmem, vmem, vmem),
        scratch_shapes=[
            pltpu.VMEM((RING * tr, hw), bf16),
            pltpu.VMEM((RING * tr, hw), bf16),
            pltpu.VMEM((RING, META, LANES), f32),
            pltpu.VMEM((slots, hw), bf16),
            pltpu.VMEM((slots, hw), bf16),
            pltpu.VMEM((slots, hw), bf16),
            pltpu.VMEM((hw, hid), bf16),
            pltpu.VMEM((hid + LANES, hw), bf16),
            pltpu.VMEM((slots, hid), f32),
            pltpu.VMEM((slots, hid), f32),
            pltpu.VMEM((slots, hid), bf16),
            pltpu.VMEM((slots, hid), bf16),
            pltpu.VMEM((slots, hid), bf16),
            pltpu.VMEM((slots, hid), bf16),
            pltpu.VMEM((COLUMNS * 16, hid), f32),
            pltpu.VMEM((COLUMNS * 16, hid), f32),
            pltpu.VMEM((COLUMNS * 16, LANES), f32),
            pltpu.VMEM((16, hw), f32),
            pltpu.VMEM((hid, slots), bf16),
            pltpu.VMEM((hid, quarter), bf16),
            pltpu.VMEM((hid, quarter), bf16),
            pltpu.VMEM((8, 2 * LANES), f32),
            pltpu.VMEM((9, 8, 2 * LANES), f32),
            pltpu.VMEM((8, 2 * LANES), f32),
            dma((5,)),
            dma((9,)), dma((9,)),
            dma((COLUMNS,)), dma((COLUMNS,)),
            dma((COLUMNS,)), dma((COLUMNS,)),
            dma((COLUMNS,)), dma((COLUMNS,)),
            dma((COLUMNS,)), dma((COLUMNS,)),
            dma((9,)), dma((9,)),
            dma((1,)), dma((1,)),
            dma((2,)), dma((2,)),
        ],
        compiler_params=pltpu.CompilerParams(
            collective_id=0, has_side_effects=True, vmem_limit_bytes=63 * 2**20
        ),
        cost_estimate=pl.CostEstimate(flops=40 * 10**9, bytes_accessed=30 * 10**6, transcendentals=10**6),
        name="routed_step",
    )(tokens, readout, meta, own, w_up[0], w_down[0])
    here = col * 16 + 12 + x
    losses = lax.dynamic_slice(small, (0, here), (1, 1)).reshape(1)
    kl_terms = lax.dynamic_slice(small, (1, here), (1, 1)).reshape(1)
    return up[None], down[None], losses, kl_terms


def solution(mesh):
    return jax.shard_map(
        local,
        mesh=mesh,
        in_specs=(
            P(("dp", "expert"), None),
            P(),
            P(("dp", "expert"), None),
            P("expert", None, None),
            P("expert", None, None),
            P(("dp", "expert"), None),
            P(("dp", "expert")),
            P(("dp", "expert")),
            P(("dp", "expert"), None),
            P(("dp", "expert")),
            P(("dp", "expert")),
        ),
        out_specs=(
            P("expert", "dp", None),
            P("expert", None, "dp"),
            P(("dp", "expert")),
            P(("dp", "expert")),
        ),
        check_vma=False,
    )
```

time: 624 us -> 304 us (0.49)
  waiting for transfers between devices: 376 us -> 0 us
  Pallas kernels: 0 us -> 285 us
  blocking collectives: 90.2 us -> 0 us
  matrix products: 55.7 us -> 0.74 us
  local copies, waits for them, and re-layouts: 52.5 us -> 6.34 us
  between operations: 18.4 us -> 4.23 us
  other arithmetic: 18.8 us -> 6.67 us
  starting transfers between devices: 11.9 us -> 0 us
    pallas_call x0 -> x1, Pallas kernels: none -> 285 us  [local(): pl.pallas_call(functools.partial(kernel, cap, hw), out_shape=(jax.ShapeDt...]
    all_to_all x1 -> x0, waiting for transfers between devices: 237 us -> none  [local(): lax.all_to_all(sent, 'expert', split_axis=0, concat_axis=0, tiled=True)]
    reduce_scatter x2 -> x0, waiting for transfers between devices: 139 us -> none  [the longest x1 79.3 us: local(): lax.psum_scatter(down_part, 'dp', scatter_dimension=1, tiled=True)[None]]
    psum x1 -> x0, blocking collectives: 90.2 us -> none  [local(): lax.psum(spread.reshape(-1), ('dp', 'expert')).reshape(replicas, 3, experts)]
    dot_general x8 -> x1, matrix products: 53.7 us -> 0.14 us  [local(): rank = jnp.dot(before, named.astype(bf16), preferred_element_type=f32)]
    reshape x6 -> x3, local copies, waits for them, and re-layouts: 23 us -> 0.01 us  [the longest x1 0.01 us: local(): by_expert = by_expert.transpose(1, 2, 0, 3).reshape(2, 2 * COLUMNS, tr)]
    slice x3 -> x0, local copies, waits for them, and re-layouts: 14.6 us -> none  [the longest x1 10.9 us: local(): y = got[:, :, width:2 * width].reshape(experts * rows, width)]
    concatenate x2 -> x0, local copies, waits for them, and re-layouts: 11.9 us -> none  [the longest x1 11.6 us: local(): sent = jnp.concatenate([sent_x, sent_y, extra], axis=2)]
  transfers between devices with their start and end apart: 3 -> 0, of which waited for: 3 -> 0; matrix products, arithmetic and copies ran while one was open for 2% -> 0% of each run, Pallas kernels for 0% -> 0%
where the time goes in v2:
time: 304 us; the launch traced here: 303 us
  Pallas kernels  285 us (94%)
  other arithmetic  6.67 us (2%)
  local copies, waits for them, and re-layouts  6.34 us (2%)
  between operations  4.23 us (1%)
    pallas_call x1, Pallas kernels, local(): pl.pallas_call(functools.partial(kernel, cap, hw), out_shape=(jax.ShapeDt...  285 us

profile of v2, /device:TPU:1, one launch (start us, length us, event | category | flops | bytes accessed | tf_op | source)
XLA Modules:
  0.0 303.4 jit_solution(6664311211803665208)
XLA Ops:
  0.6 0.0 copy-start
  0.6 0.0 copy-start.2
  2.9 1.3 reduce_sum.39
  4.2 0.7 fusion.1
  4.9 0.1 select_bitcast_fusion
  5.0 0.8 convert_reduce_fusion.1
  5.8 3.0 %fusion = (f32[]{:T(128)}, f32[5120]{0:T(1024)S(1)}) fusion(bf16[128,5120]{1,0:T(8,128)(2,1)} %tok.1, bf16[128,5120]{1,0:T(8,128)(2,1)} %rdo.1), kind=kLoop, calls=%fused_computation.2 | loop fusion | flops 3271679 | bytes 2641924 | tf_op jit(solution)/shard_map/reduce_sum | solution.py:426
  10.2 0.1 pad_maximum_fusion.2
  10.2 0.1 broadcast_select_fusion
  10.3 0.6 pad.9.own
  10.9 0.0 copy-done
  10.9 0.0 copy-done.2
  10.9 0.6 fusion.6
  11.6 0.7 pad_maximum_fusion.meta
  12.3 285.4 %routed_step.1 = (bf16[1280,768]{1,0:T(8,128)(2,1)}, bf16[768,1280]{1,0:T(8,128)(2,1)}, f32[8,256]{1,0:T(8,128)}) custom-call(bf16[128,5120]{1,0:T(8,128)(2,1)} %tok.1, bf16[128,5120]{1,0:T(8,128)(2,1)} %rdo.1, f32[4,80,128]{2,1,0:T(8,128)} %pad_maximum_fusion.meta, f32[8,256]{1,0:T(8,128)} %pad.9.own, bf16[5120,768]{1,0:T(8,128)(2,1)} %bitcast.31, ...), custom_call_target="tpu_custom_call" | custom-call | flops 40000000000 | bytes 30000000 | tf_op jit(solution)/shard_map/routed_step/pallas_call | solution.py:451
  297.7 1.3 constant_dynamic-slice_fusion
  299.0 0.0 copy-start.1
  299.0 3.1 %copy.25 = bf16[1,1280,768]{2,1,0:T(8,128)(2,1)} copy(bf16[1,1280,768]{2,1,0:T(8,128)(2,1)} %bitcast.28) | data formatting | bytes 3932160
  302.1 0.0 copy-done.1
  302.1 1.3 copy.26
  (10 shorter events, 0.0 us)
Async XLA Ops:
  0.6 10.3 %copy-start = (bf16[128,5120]{1,0:T(8,128)(2,1)S(1)}, bf16[128,5120]{1,0:T(8,128)(2,1)}, u32[]{:S(2)}) copy-start(bf16[128,5120]{1,0:T(8,128)(2,1)} %tok.1) | copy-start | bytes 3932164
  0.6 10.3 %copy-start.2 = (bf16[5120,160]{0,1:T(8,128)(2,1)S(1)}, bf16[5120,160]{0,1:T(8,128)(2,1)}, u32[]{:S(2)}) copy-start(bf16[5120,160]{0,1:T(8,128)(2,1)} %param.12) | copy-start | bytes 4915204
  299.0 3.1 %copy-start.1 = (bf16[768,1280]{1,0:T(8,128)(2,1)S(1)}, bf16[768,1280]{1,0:T(8,128)(2,1)}, u32[]{:S(2)}) copy-start(bf16[768,1280]{1,0:T(8,128)(2,1)} %get-tuple-element.8) | copy-start | bytes 5898244

commit v3 on v2

v3 whole, which is shorter than its diff:
```python
import functools

import jax
import jax.numpy as jnp
from jax import lax
from jax.experimental import pallas as pl
from jax.experimental.pallas import tpu as pltpu
from jax.sharding import PartitionSpec as P

MESH = pl.DeviceIdType.MESH
routed_scale = 16.0
kto_beta = 0.1
loss_scale = 1024.0
f32, bf16 = jnp.float32, jnp.bfloat16

RING = 4
COLUMNS = 16
LANES = 128
META = 80
PARTS = (32, 32, 16)
PART_AT = (0, 32, 64)
NT = (((1,), (1,)), ((), ()))
TN = (((0,), (0,)), ((), ()))


def split3(value):
    high = value.astype(bf16).astype(f32)
    middle = (value - high).astype(bf16).astype(f32)
    low = (value - high - middle).astype(bf16).astype(f32)
    return high, middle, low


def place():
    dp, ex = lax.axis_index("dp"), lax.axis_index("expert")
    return dp // 2, dp % 2, ex % 2, ex // 2


def kernel(
    cap, hw, tok, rdo, meta, own, wu_hbm, wd_hbm,
    up_hbm, down_hbm, small_out,
    xb, yb, mb, ob, xin, yin, m1x, m2x, m1y, m2y, wu, wd, pa, ra, pas, pap, ras, rap, prs, hst, wst,
    exty, acc, arb, arc,
    lsem, osem, ag_s, ag_r, a1s, a1r, a2s, a2r, b1s, b1r, b2s, b2r, ds, dr,
    ps, pr, qs, qr, ar_s, ar_r, c_s, c_r, g_s, g_r,
):
    rb = META
    tr = tok.shape[0]
    hid = wu.shape[1]
    slots = COLUMNS * rb
    x_lo, core, x_hi, col = place()
    dp, ex = lax.axis_index("dp"), lax.axis_index("expert")
    x = x_hi * 2 + x_lo
    y, z = col % RING, col // RING
    mid = hw // 2

    def dev_x(xx):
        return ((xx % 2) * 2 + core, col * 2 + xx // 2)

    def dev_col(cc):
        return (dp, cc * 2 + x_hi)

    sibling = (x_lo * 2 + 1 - core, ex)
    partner = ((1 - x_lo) * 2 + core, ex)

    def plus(dz, dy):
        return ((z + dz) % RING) * RING + (y + dy) % RING

    def minus(dz, dy):
        return ((z + RING - dz) % RING) * RING + (y + RING - dy) % RING

    def rows(start, size):
        return pl.ds(pl.multiple_of(start, 16), size)

    def remote(src, dst, ss, rs, dev):
        return pltpu.make_async_remote_copy(
            src_ref=src, dst_ref=dst, send_sem=ss, recv_sem=rs, device_id=dev, device_id_type=MESH
        )

    def loop(count, body, start=0):
        def step(i, carry):
            body(i)
            return carry

        lax.fori_loop(start, count, step, 0)

    barrier = pltpu.get_barrier_semaphore()

    def greet(dev):
        pl.semaphore_signal(barrier, inc=1, device_id=dev, device_id_type=MESH)

    loop(RING, lambda d: greet(dev_x((x + d) % RING)), 1)
    loop(RING, lambda d: greet(dev_col(plus(d, 0))), 1)
    loop(RING, lambda d: greet(dev_col(plus(0, d))), 1)
    greet(sibling)
    half = pl.ds(pl.multiple_of(x_lo * hw, LANES), hw)
    mine = pl.ds(pl.multiple_of(x * tr, LANES), tr)
    locals_ = [
        pltpu.make_async_copy(tok.at[:, half], xb.at[mine], lsem.at[0]),
        pltpu.make_async_copy(rdo.at[:, half], yb.at[mine], lsem.at[1]),
        pltpu.make_async_copy(meta.at[x], mb.at[x], lsem.at[2]),
        pltpu.make_async_copy(wu_hbm.at[half], wu, lsem.at[3]),
        pltpu.make_async_copy(wd_hbm.at[:, half], wd.at[pl.ds(0, hid)], lsem.at[4]),
    ]
    for copy in locals_:
        copy.start()
    pl.semaphore_wait(barrier, 3 * (RING - 1) + 1)

    pieces = ((0, 0, hw), (1, 0, mid), (1, mid, mid), (2, 0, hw))

    def ring_copy(which, d):
        to = (x + d) % RING
        kind, start, size = pieces[which]
        cols = pl.ds(pl.multiple_of((to % 2) * hw + start, LANES), size)
        here = pl.ds(start, size)
        src = (meta.at[to], tok.at[:, cols], rdo.at[:, cols])[kind]
        dst = (mb.at[x], xb.at[mine, here], yb.at[mine, here])[kind]
        return remote(src, dst, ag_s.at[which * 3 + d - 1], ag_r.at[which * 3 + d - 1], dev_x(to))

    rings = [[ring_copy(which, d) for d in (1, 3, 2)] for which in range(4)]

    def start_ring(which):
        for copy in rings[which]:
            copy.start()

    def wait_ring(which):
        for copy in rings[which]:
            copy.wait_recv()

    start_ring(0)
    start_ring(1)
    for copy in locals_:
        copy.wait()
    wait_ring(0)

    exty[...] = jnp.zeros_like(exty)
    tall = lax.broadcasted_iota(jnp.int32, (LANES, LANES), 0)
    for j in range(hw // LANES):
        lane = pl.ds(j * LANES, LANES)
        for b in range(RING):
            exty[12 + b : 13 + b, lane] = mb[b, 32 + j : 33 + j, :]
        terms = split3(mb[x, 52 + j : 53 + j, :]) + split3(mb[x + 1 - 2 * x_lo, 52 + j : 53 + j, :])
        block = jnp.zeros((LANES, LANES), f32)
        for i, term in enumerate(terms):
            block = jnp.where(tall == i, term, block)
        wd[pl.ds(hid, LANES), lane] = block.astype(bf16)

    def shipment(n):
        if n < 2:
            return rb, 0, n * mid, mid, 0, n * (mid // 2), m1x, m2x, xin
        size, at = PARTS[n - 2], PART_AT[n - 2]
        return size, at * COLUMNS, 0, hw, at * 9, 0, m1y, m2y, yin

    def block(n, cc):
        size, base = shipment(n)[:2]
        return rows(base + cc * size, size)

    def halves(n):
        start, width = shipment(n)[2:4]
        return pl.ds(start, width // 2), pl.ds(start + width // 2, width // 2), pl.ds(start, width)

    def held(n, i):
        size, _, _, width, base, at = shipment(n)[:6]
        return rows(base + i * size, size), pl.ds(at, width // 2)

    def turn(i):
        return 1 + i // 3, 1 + i % 3

    def a_first(n, i):
        dz, dy = turn(i)
        there = held(n, i)
        return remote(
            ob.at[block(n, plus(dz, dy)), halves(n)[0]], shipment(n)[6].at[there[0], there[1]],
            a1s.at[n, i], a1r.at[n, i], dev_col(plus(0, dy)),
        )

    def a_second(n, i):
        dz, dy = turn(i)
        there = held(n, i)
        return remote(
            shipment(n)[6].at[there[0], there[1]], shipment(n)[8].at[block(n, minus(0, dy)), halves(n)[0]],
            a2s.at[n, i], a2r.at[n, i], dev_col(plus(dz, 0)),
        )

    def b_first(n, i):
        dz, dy = turn(i)
        there = held(n, i)
        return remote(
            ob.at[block(n, plus(dz, dy)), halves(n)[1]], shipment(n)[7].at[there[0], there[1]],
            b1s.at[n, i], b1r.at[n, i], dev_col(plus(dz, 0)),
        )

    def b_second(n, i):
        dz, dy = turn(i)
        there = held(n, i)
        return remote(
            shipment(n)[7].at[there[0], there[1]], shipment(n)[8].at[block(n, minus(dz, 0)), halves(n)[1]],
            b2s.at[n, i], b2r.at[n, i], dev_col(plus(0, dy)),
        )

    def straight(n, i):
        dz, dy = (i + 1) * (1 - i // 3), (i - 2) * (i // 3)
        to = plus(dz, dy)
        return remote(
            ob.at[block(n, to), halves(n)[2]], shipment(n)[8].at[block(n, col), halves(n)[2]],
            ds.at[n, i], dr.at[n, i], dev_col(to),
        )

    def keep(n):
        cols = halves(n)[2]
        return pltpu.make_async_copy(ob.at[block(n, col), cols], shipment(n)[8].at[block(n, col), cols], osem.at[n])

    wide = 512

    def picks(cc, start, size):
        want = jnp.concatenate([mb[b, pl.ds(cc, 1), :] for b in range(RING)], axis=1)
        row = start + lax.broadcasted_iota(jnp.int32, (size, RING * tr), 0).astype(f32)
        return jnp.where(row == want, 1.0, 0.0).astype(bf16)

    def gate_rows(cc):
        gate = jnp.concatenate([mb[b, pl.ds(16 + cc, 1), :] for b in range(RING)], axis=1)
        row = lax.broadcasted_iota(jnp.int32, (16, RING * tr), 0)
        lifted = jnp.zeros((16, RING * tr), f32)
        for i, term in enumerate(split3(gate)):
            lifted = jnp.where(row == 12 + i, term, lifted)
        gates = lax.dot_general(lifted.astype(bf16), picks(cc, 0, LANES), NT, preferred_element_type=f32)
        pair = [sum(mb[b, 72 + i : 73 + i, :] for b in range(RING)) for i in range(2)]
        pair = jnp.concatenate(pair, axis=1)
        gates = jnp.concatenate([gates, jnp.zeros((16, LANES), f32)], axis=1)
        last = lax.broadcasted_iota(jnp.int32, (16, 2 * LANES), 0) == 15
        return gates + jnp.where(last, pair, 0.0)

    def build(n):
        size, base, start, width = shipment(n)[:4]
        at = 0 if n < 2 else PART_AT[n - 2]
        source = xb if n < 2 else yb

        def plane(zz):
            pick = jnp.concatenate([picks(zz * RING + i, at, size) for i in range(RING)], axis=0)
            place_ = rows(base + zz * (RING * size), RING * size)
            for lo in range(start, start + width, wide):
                lane = pl.ds(lo, min(wide, start + width - lo))
                made = jnp.dot(pick, source[:, lane], preferred_element_type=f32)
                if n == 4:
                    made = made + jnp.concatenate([exty[:, lane]] * RING, axis=0)
                ob[place_, lane] = made.astype(bf16)
            if n == 0:
                for i in range(RING):
                    tail = rows(zz * (RING * size) + i * size + 64, 16)
                    first = pl.ds(0, 2 * LANES)
                    ob[tail, first] = (ob[tail, first].astype(f32) + gate_rows(zz * RING + i)).astype(bf16)

        def go(k):
            dz = (k + 1) % RING
            plane((z + dz) % RING)

            @pl.when(dz > 0)
            def _():
                for dy in range(1, RING):
                    i = (dz - 1) * 3 + dy - 1
                    a_first(n, i).start()
                    b_first(n, i).start()
                straight(n, dz - 1).start()

            @pl.when(dz == 0)
            def _():
                for dy in range(1, RING):
                    straight(n, 2 + dy).start()
                keep(n).start()

        loop(RING, go)

    def forward(n):
        def go(i):
            a_first(n, i).wait_recv()
            a_second(n, i).start()
            b_first(n, i).wait_recv()
            b_second(n, i).start()

        loop(9, go)

    def built_sent(n):
        def go(i):
            a_first(n, i).wait_send()
            b_first(n, i).wait_send()

        loop(9, go)
        loop(6, lambda i: straight(n, i).wait_send())
        if n < 2:
            keep(n).wait()

    def forwards_sent(n):
        def go(i):
            a_second(n, i).wait_send()
            b_second(n, i).wait_send()

        loop(9, go)

    def arrived(n):
        def go(i):
            a_second(n, i).wait_recv()
            b_second(n, i).wait_recv()

        loop(9, go)
        loop(6, lambda i: straight(n, i).wait_recv())
        if n >= 2:
            keep(n).wait()

    span = 256

    def pair_x(j):
        at = rows(j * span, span)
        return remote(pas.at[at], pap.at[at], ps.at[j], pr.at[j], partner)

    def pair_y(j):
        at = rows(j * span, span)
        return remote(ras.at[at], rap.at[at], qs.at[j], qr.at[j], partner)

    def use_x(j):
        at = rows(j * span, span)
        part = jnp.dot(xin[at, :], wu[...], preferred_element_type=f32)
        pa[at, :] = part
        pas[at, :] = part.astype(bf16)
        pair_x(j).start()

    def use_y(j):
        at = rows(j * span, span)
        part = lax.dot_general(yin[at, :], wd[pl.ds(0, hid), :], NT, preferred_element_type=f32)
        ra[at, :] = part
        ras[at, :] = part.astype(bf16)
        pair_y(j).start()

    acc[...] = own[...]

    def meet(p):
        size, at = PARTS[p], PART_AT[p]
        shape = (size, 2 * LANES)
        lane = lax.broadcasted_iota(jnp.int32, shape, 1)
        row = at + lax.broadcasted_iota(jnp.int32, shape, 0)
        row_lane = jnp.where(row < RING * cap, 12 + row // cap, -1)
        square = at + lax.broadcasted_iota(jnp.int32, (size, LANES), 0) == lax.broadcasted_iota(
            jnp.int32, (size, LANES), 1
        )
        first = lax.broadcasted_iota(jnp.int32, (16, size), 0)
        which = (at + lax.broadcasted_iota(jnp.int32, (16, size), 1)) // cap
        gather = jnp.where(first == which, 1.0, 0.0).astype(bf16)

        def go(cc):
            xr_ = rows(cc * rb + at, size)
            yr_ = rows(at * COLUMNS + cc * size, size)
            tail = xin[rows(cc * rb + 64, 16), pl.ds(0, 2 * LANES)].astype(f32)
            p_ = pa[xr_, :] + pap[xr_, :].astype(f32)
            r = ra[yr_, :] + rap[yr_, :].astype(f32)
            gate = jnp.sum(tail[12:15, :LANES], axis=0, keepdims=True)
            gate = jnp.sum(jnp.where(square, gate, 0.0), axis=1, keepdims=True)
            logistic = jax.nn.sigmoid(p_)
            gated = gate * (p_ * logistic)
            ra[yr_, :] = gated
            pa[xr_, :] = gate * r * (logistic * (1.0 + p_ * (1.0 - logistic)))
            margin = jnp.sum(gated * r, axis=1, keepdims=True)
            hot = jnp.where(lane - cc * 16 == row_lane, 1.0, 0.0)
            acc[1:2, :] += 0.5 * jnp.sum(hot * margin, axis=0, keepdims=True)
            spot = rows(cc * 16, 16)
            summed = jnp.dot(gather, gated.astype(bf16), preferred_element_type=f32)
            if p == 0:
                acc[3:4, :] += tail[15:16]
                hst[spot, :] = summed
            else:
                hst[spot, :] += summed
            if p == 2:
                prs[spot, :] = r

        loop(COLUMNS, go)

    wait_ring(1)
    start_ring(2)
    build(0)
    wait_ring(2)
    start_ring(3)
    build(1)
    forward(0)
    built_sent(0)
    forward(1)
    built_sent(1)
    wait_ring(3)
    build(2)
    build(3)
    arrived(0)
    arrived(1)
    loop(5, use_x)
    forward(2)
    build(4)
    forward(3)
    arrived(2)
    loop(2, use_y)
    forward(4)
    arrived(3)
    loop(4, use_y, 2)
    loop(5, lambda j: pair_x(j).wait_recv())
    loop(2, lambda j: pair_y(j).wait_recv())
    meet(0)
    arrived(4)
    last_at = rows(4 * span, span)
    last_part = lax.dot_general(yin[last_at, :], wd[...], NT, preferred_element_type=f32)
    ra[last_at, :] = last_part[:, :hid]
    ras[last_at, :] = last_part[:, :hid].astype(bf16)
    pair_y(4).start()
    wst[...] = last_part[:, hid:]
    loop(4, lambda j: pair_y(j).wait_recv(), 2)
    meet(1)
    pair_y(4).wait_recv()
    meet(2)

    wide_t = wst[...].T
    base_own = wide_t[0:1] + wide_t[1:2] + wide_t[2:3]
    base_other = wide_t[3:4] + wide_t[4:5] + wide_t[5:6]
    pairs = acc[3:4, :]
    terms = 0.5 * lax.dot_general(
        hst[...], prs[...], NT, precision=lax.Precision.HIGHEST, preferred_element_type=f32
    )
    named = lax.broadcasted_iota(jnp.int32, terms.shape, 0)
    terms += jnp.where(named == col * 16 + x, base_own, 0.0)
    terms += jnp.where(named == col * 16 + x + 1 - 2 * x_lo, base_other, 0.0)
    used = lax.broadcasted_iota(jnp.int32, (1, 2 * LANES), 1) % 16 >= 12
    chosen = jnp.where((named.astype(f32) == pairs) & used, terms, 0.0)
    acc[0:1, :] += jnp.sum(chosen, axis=0, keepdims=True)

    def ring_sum(axis, dev):
        copies = [
            remote(acc, arb.at[axis * 3 + d - 1], ar_s.at[axis * 3 + d - 1], ar_r.at[axis * 3 + d - 1], dev(d))
            for d in (1, 3, 2)
        ]
        for copy in copies:
            copy.start()
        for copy in copies:
            copy.wait()
        acc[...] = acc[...] + arb[axis * 3] + arb[axis * 3 + 1] + arb[axis * 3 + 2]

    ring_sum(0, lambda d: dev_x((x + d) % RING))
    ring_sum(1, lambda d: dev_col(plus(0, d)))
    ring_sum(2, lambda d: dev_col(plus(d, 0)))
    for n in range(2, 5):
        built_sent(n)
    for n in range(5):
        forwards_sent(n)
    loop(5, lambda j: pair_x(j).wait_send())
    loop(5, lambda j: pair_y(j).wait_send())
    for ring in rings:
        for copy in ring:
            copy.wait_send()
    swap = remote(acc, arc, c_s.at[0], c_r.at[0], sibling)
    swap.start()
    swap.wait()
    kl_row = jnp.where(used, acc[0:1, :], 0.0)
    kl_other = jnp.where(used, arc[0:1, :], 0.0)
    count = RING * COLUMNS * 2
    anchor = jnp.sum(kl_row + kl_other, axis=1, keepdims=True) / count
    signed = acc[2:3, :]
    kept = jax.nn.sigmoid(kto_beta * signed * (acc[1:2, :] - anchor))
    slope = -loss_scale * kto_beta * signed * kept * (1.0 - kept)
    small_out[...] = jnp.zeros_like(small_out)
    small_out[0:1, :] = 1.0 - kept
    small_out[1:2, :] = kl_row

    def scaled(source, dst, start, size, at):
        lane = lax.broadcasted_iota(jnp.int32, (size, 2 * LANES), 1)
        row = at + lax.broadcasted_iota(jnp.int32, (size, 2 * LANES), 0)
        row_lane = jnp.where(row < RING * cap, 12 + row // cap, -1)

        def go(cc):
            here = rows(start + cc * size, size)
            factor = jnp.sum(jnp.where(lane - cc * 16 == row_lane, slope, 0.0), axis=1, keepdims=True)
            dst[here, :] = (source[here, :] * factor).astype(bf16)

        loop(COLUMNS, go)

    quarter = hw // 2
    step = 256
    other = (1 - core) * quarter
    this = core * quarter
    hid_t = m2y.at[pl.ds(0, hid)]
    up_got, down_got = rap, m1y.at[pl.ds(0, hid)]
    up_out, down_out = pl.ds(0, hid), m1x.at[pl.ds(0, hid)]
    down_sent = pl.ds(quarter, quarter)

    def up_block(start, j):
        at = pl.ds(pl.multiple_of(start + j * step, LANES), step)
        return lax.dot_general(xin[:, at], pas[...], TN, preferred_element_type=f32)

    def down_block(start, j):
        at = pl.ds(pl.multiple_of(start + j * step, LANES), step)
        return jnp.dot(hid_t[...], yin[:, at], preferred_element_type=f32)

    def piece(j, base=0):
        return pl.ds(pl.multiple_of(base + j * step, step), step)

    def other_up(j):
        pap[piece(j), :] = up_block(other, j).astype(bf16)

    def other_down(j):
        ob[pl.ds(0, hid), piece(j, quarter)] = down_block(other, j).astype(bf16)

    def this_up(j):
        ob[piece(j), up_out] = (up_block(this, j) + up_got[piece(j), :].astype(f32)).astype(bf16)

    def this_down(j):
        down_out[:, piece(j)] = (down_block(this, j) + down_got[:, piece(j)].astype(f32)).astype(bf16)

    up_copy = remote(pap, up_got, g_s.at[0], g_r.at[0], sibling)
    down_copy = remote(ob.at[pl.ds(0, hid), down_sent], down_got, g_s.at[1], g_r.at[1], sibling)
    blocks = quarter // step
    scaled(pa, pas, 0, rb, 0)
    loop(blocks, other_up)
    up_copy.start()
    for p in range(3):
        scaled(ra, ras, PART_AT[p] * COLUMNS, PARTS[p], PART_AT[p])
    for j in range(slots // step):
        at = pl.ds(j * step, step)
        hid_t[:, at] = ras[at, :].T
    loop(blocks, other_down)
    down_copy.start()
    up_copy.wait_recv()
    loop(blocks, this_up)
    up_done = pltpu.make_async_copy(ob.at[pl.ds(0, quarter), up_out], up_hbm, lsem.at[0])
    up_done.start()
    down_copy.wait_recv()
    loop(blocks, this_down)
    down_done = pltpu.make_async_copy(down_out, down_hbm, lsem.at[1])
    down_done.start()
    up_copy.wait_send()
    down_copy.wait_send()
    up_done.wait()
    down_done.wait()


def local(
    tokens, router, expert_ids, w_up, w_down, readout, ref_logp, labels, prompt_read, kl_pair, kl_ref
):
    experts = lax.axis_size("expert")
    tr, width = tokens.shape
    top = expert_ids.shape[1]
    cap = 4 * tr * top // (5 * experts)
    hid = w_up.shape[2]
    hw = width // 2
    x_lo, core, x_hi, col = place()
    x = x_hi * 2 + x_lo

    logits = jnp.dot(tokens, router, preferred_element_type=f32)
    scores = jnp.exp(logits)
    gates = routed_scale * (scores / jnp.sum(scores, axis=1, keepdims=True))[:, :experts]
    named = jnp.any(expert_ids[:, :, None] == jnp.arange(experts, dtype=jnp.int32), axis=1)
    before = (jnp.arange(tr)[:, None] > jnp.arange(tr)[None, :]).astype(bf16)
    rank = jnp.dot(before, named.astype(bf16), preferred_element_type=f32)
    want = jnp.where(named & (rank < cap), rank + (cap * x).astype(f32), -1.0)
    by_expert = jnp.stack([want, gates]).transpose(2, 0, 1).reshape(COLUMNS, 2, 2, tr)
    by_expert = by_expert.transpose(1, 2, 0, 3).reshape(2, 2 * COLUMNS, tr)

    tokens_f = tokens.astype(f32)
    own_margin = jnp.sum(tokens_f * readout.astype(f32)) - jnp.sum(ref_logp)
    base = jnp.sum(tokens_f, axis=0).reshape(2, hw // LANES, LANES)
    prompt = prompt_read.astype(f32).reshape(2, hw // LANES, LANES)
    lane = jnp.arange(2 * LANES)
    spot = lane == col * 16 + 12 + x
    pair = (kl_pair[0] // 2) * 16 + (kl_pair[0] % 2) * 2 + x_lo
    misc = jnp.pad(jnp.where(spot, pair, 0).astype(f32).reshape(2, LANES), ((0, 6), (0, 0)))
    per_half = jnp.concatenate([prompt, base], axis=1)
    meta = jnp.concatenate(
        [
            jnp.repeat(by_expert, 2, axis=0),
            jnp.concatenate([per_half, per_half], axis=0),
            jnp.broadcast_to(misc, (RING, 8, LANES)),
        ],
        axis=1,
    )
    sign = jnp.where(labels[0] == 1, 1.0, -1.0)
    own = jnp.where(spot[None, :], jnp.stack([-kl_ref[0], own_margin, sign])[:, None], 0.0)
    own = jnp.pad(own, ((0, 5), (0, 0)))

    slots = COLUMNS * META
    quarter = hw // 2
    dma = pltpu.SemaphoreType.DMA
    any_ = pl.BlockSpec(memory_space=pl.ANY)
    vmem = pl.BlockSpec(memory_space=pltpu.VMEM)
    up, down, small = pl.pallas_call(
        functools.partial(kernel, cap, hw),
        out_shape=(
            jax.ShapeDtypeStruct((quarter, hid), bf16),
            jax.ShapeDtypeStruct((hid, quarter), bf16),
            jax.ShapeDtypeStruct((8, 2 * LANES), f32),
        ),
        in_specs=[any_, any_, any_, vmem, any_, any_],
        out_specs=(any_, any_, vmem),
        scratch_shapes=[
            pltpu.VMEM((RING * tr, hw), bf16),
            pltpu.VMEM((RING * tr, hw), bf16),
            pltpu.VMEM((RING, META, LANES), f32),
            pltpu.VMEM((slots, hw), bf16),
            pltpu.VMEM((slots, hw), bf16),
            pltpu.VMEM((slots, hw), bf16),
            pltpu.VMEM((max(9 * META, hid), quarter), bf16),
            pltpu.VMEM((9 * META, quarter), bf16),
            pltpu.VMEM((max(9 * META, hid), quarter), bf16),
            pltpu.VMEM((max(9 * META, hid), quarter), bf16),
            pltpu.VMEM((hw, hid), bf16),
            pltpu.VMEM((hid + LANES, hw), bf16),
            pltpu.VMEM((slots, hid), f32),
            pltpu.VMEM((slots, hid), f32),
            pltpu.VMEM((slots, hid), bf16),
            pltpu.VMEM((slots, hid), bf16),
            pltpu.VMEM((slots, hid), bf16),
            pltpu.VMEM((slots, hid), bf16),
            pltpu.VMEM((COLUMNS * 16, hid), f32),
            pltpu.VMEM((COLUMNS * 16, hid), f32),
            pltpu.VMEM((COLUMNS * 16, LANES), f32),
            pltpu.VMEM((16, hw), f32),
            pltpu.VMEM((8, 2 * LANES), f32),
            pltpu.VMEM((9, 8, 2 * LANES), f32),
            pltpu.VMEM((8, 2 * LANES), f32),
            dma((5,)), dma((5,)),
            dma((12,)), dma((12,)),
        ]
        + [dma((5, 9)) for _ in range(8)]
        + [dma((5, 6)) for _ in range(2)]
        + [
            dma((5,)), dma((5,)),
            dma((5,)), dma((5,)),
            dma((9,)), dma((9,)),
            dma((1,)), dma((1,)),
            dma((2,)), dma((2,)),
        ],
        compiler_params=pltpu.CompilerParams(
            collective_id=0, has_side_effects=True, vmem_limit_bytes=63 * 2**20
        ),
        cost_estimate=pl.CostEstimate(flops=40 * 10**9, bytes_accessed=30 * 10**6, transcendentals=10**6),
        name="routed_step",
    )(tokens, readout, meta, own, w_up[0], w_down[0])
    here = col * 16 + 12 + x
    losses = lax.dynamic_slice(small, (0, here), (1, 1)).reshape(1)
    kl_terms = lax.dynamic_slice(small, (1, here), (1, 1)).reshape(1)
    return up[None], down[None], losses, kl_terms


def solution(mesh):
    return jax.shard_map(
        local,
        mesh=mesh,
        in_specs=(
            P(("dp", "expert"), None),
            P(),
            P(("dp", "expert"), None),
            P("expert", None, None),
            P("expert", None, None),
            P(("dp", "expert"), None),
            P(("dp", "expert")),
            P(("dp", "expert")),
            P(("dp", "expert"), None),
            P(("dp", "expert")),
            P(("dp", "expert")),
        ),
        out_specs=(
            P("expert", "dp", None),
            P("expert", None, "dp"),
            P(("dp", "expert")),
            P(("dp", "expert")),
        ),
        check_vma=False,
    )
```

time: 304 us -> 256 us (0.84)
  Pallas kernels: 285 us -> 238 us
    pallas_call x1, Pallas kernels: 285 us -> 238 us  [local(): pl.pallas_call(functools.partial(kernel, cap, hw), out_shape=(jax.ShapeDt...]
where the time goes in v3:
time: 256 us
  Pallas kernels  238 us (93%)
  other arithmetic  6.67 us (3%)
  local copies, waits for them, and re-layouts  6.34 us (2%)
  between operations  4.23 us (2%)
    pallas_call x1, Pallas kernels, local(): pl.pallas_call(functools.partial(kernel, cap, hw), out_shape=(jax.ShapeDt...  238 us

profile of v3, /device:TPU:1, one launch (start us, length us, event | category | flops | bytes accessed | tf_op | source)
XLA Modules:
  0.0 255.8 jit_solution(5660591056451621239)
XLA Ops:
  0.6 0.0 copy-start
  0.6 0.0 copy-start.2
  2.9 1.3 reduce_sum.39
  4.2 0.7 fusion.1
  4.9 0.1 select_bitcast_fusion
  5.0 0.8 convert_reduce_fusion.1
  5.8 3.0 %fusion = (f32[]{:T(128)}, f32[5120]{0:T(1024)S(1)}) fusion(bf16[128,5120]{1,0:T(8,128)(2,1)} %tok.1, bf16[128,5120]{1,0:T(8,128)(2,1)} %rdo.1), kind=kLoop, calls=%fused_computation.2 | loop fusion | flops 3271679 | bytes 2641924 | tf_op jit(solution)/shard_map/reduce_sum | solution.py:558
  10.2 0.1 pad_maximum_fusion.2
  10.2 0.1 broadcast_select_fusion
  10.3 0.6 pad.9.own
  10.9 0.0 copy-done
  10.9 0.0 copy-done.2
  10.9 0.6 fusion.6
  11.6 0.7 pad_maximum_fusion.meta
  12.3 237.8 %routed_step.1 = (bf16[1280,768]{1,0:T(8,128)(2,1)}, bf16[768,1280]{1,0:T(8,128)(2,1)}, f32[8,256]{1,0:T(8,128)}) custom-call(bf16[128,5120]{1,0:T(8,128)(2,1)} %tok.1, bf16[128,5120]{1,0:T(8,128)(2,1)} %rdo.1, f32[4,80,128]{2,1,0:T(8,128)} %pad_maximum_fusion.meta, f32[8,256]{1,0:T(8,128)} %pad.9.own, bf16[5120,768]{1,0:T(8,128)(2,1)} %bitcast.31, ...), custom_call_target="tpu_custom_call" | custom-call | flops 40000000000 | bytes 30000000 | tf_op jit(solution)/shard_map/routed_step/pallas_call | solution.py:583
  250.1 1.3 constant_dynamic-slice_fusion
  251.4 0.0 copy-start.1
  251.4 3.1 %copy.25 = bf16[1,1280,768]{2,1,0:T(8,128)(2,1)} copy(bf16[1,1280,768]{2,1,0:T(8,128)(2,1)} %bitcast.28) | data formatting | bytes 3932160
  254.5 0.0 copy-done.1
  254.5 1.3 copy.26
  (10 shorter events, 0.0 us)
Async XLA Ops:
  0.6 10.3 %copy-start = (bf16[128,5120]{1,0:T(8,128)(2,1)S(1)}, bf16[128,5120]{1,0:T(8,128)(2,1)}, u32[]{:S(2)}) copy-start(bf16[128,5120]{1,0:T(8,128)(2,1)} %tok.1) | copy-start | bytes 3932164
  0.6 10.3 %copy-start.2 = (bf16[5120,160]{0,1:T(8,128)(2,1)S(1)}, bf16[5120,160]{0,1:T(8,128)(2,1)}, u32[]{:S(2)}) copy-start(bf16[5120,160]{0,1:T(8,128)(2,1)} %param.12) | copy-start | bytes 4915204
  251.4 3.1 %copy-start.1 = (bf16[768,1280]{1,0:T(8,128)(2,1)S(1)}, bf16[768,1280]{1,0:T(8,128)(2,1)}, u32[]{:S(2)}) copy-start(bf16[768,1280]{1,0:T(8,128)(2,1)} %get-tuple-element.8) | copy-start | bytes 5898244

commit v4 on v3

--- a/solution.py
+++ b/solution.py
@@ -19,6 +19,7 @@
 META = 80
 PARTS = (32, 32, 16)
 PART_AT = (0, 32, 64)
+CUTS = ((0, 512), (512, 1024), (1536, 1024))
 NT = (((1,), (1,)), ((), ()))
 TN = (((0,), (0,)), ((), ()))
 
@@ -36,10 +37,10 @@
 
 
 def kernel(
-    cap, hw, tok, rdo, meta, own, wu_hbm, wd_hbm,
+    cap, hw, tok, rdo, route, ids, logp, prompt, label, mate, klr, wu_hbm, wd_hbm,
     up_hbm, down_hbm, small_out,
     xb, yb, mb, ob, xin, yin, m1x, m2x, m1y, m2y, wu, wd, pa, ra, pas, pap, ras, rap, prs, hst, wst,
-    exty, acc, arb, arc,
+    exty, meta, gsc, acc, arb, arc,
     lsem, osem, ag_s, ag_r, a1s, a1r, a2s, a2r, b1s, b1r, b2s, b2r, ds, dr,
     ps, pr, qs, qr, ar_s, ar_r, c_s, c_r, g_s, g_r,
 ):
@@ -51,7 +52,6 @@
     dp, ex = lax.axis_index("dp"), lax.axis_index("expert")
     x = x_hi * 2 + x_lo
     y, z = col % RING, col // RING
-    mid = hw // 2
 
     def dev_x(xx):
         return ((xx % 2) * 2 + core, col * 2 + xx // 2)
@@ -93,19 +93,24 @@
     loop(RING, lambda d: greet(dev_col(plus(0, d))), 1)
     greet(sibling)
     half = pl.ds(pl.multiple_of(x_lo * hw, LANES), hw)
+    away = pl.ds(pl.multiple_of((1 - x_lo) * hw, LANES), hw)
     mine = pl.ds(pl.multiple_of(x * tr, LANES), tr)
+    routes = route.shape[0]
     locals_ = [
         pltpu.make_async_copy(tok.at[:, half], xb.at[mine], lsem.at[0]),
         pltpu.make_async_copy(rdo.at[:, half], yb.at[mine], lsem.at[1]),
-        pltpu.make_async_copy(meta.at[x], mb.at[x], lsem.at[2]),
-        pltpu.make_async_copy(wu_hbm.at[half], wu, lsem.at[3]),
-        pltpu.make_async_copy(wd_hbm.at[:, half], wd.at[pl.ds(0, hid)], lsem.at[4]),
+        pltpu.make_async_copy(tok.at[:, away], ob.at[pl.ds(0, tr)], lsem.at[2]),
+        pltpu.make_async_copy(route.at[:, half], ob.at[pl.ds(2 * tr, routes)], lsem.at[3]),
+        pltpu.make_async_copy(route.at[:, away], ob.at[pl.ds(2 * tr + routes, routes)], lsem.at[4]),
+        pltpu.make_async_copy(rdo.at[:, away], ob.at[pl.ds(tr, tr)], lsem.at[5]),
+        pltpu.make_async_copy(wu_hbm.at[half], wu, lsem.at[6]),
+        pltpu.make_async_copy(wd_hbm.at[:, half], wd.at[pl.ds(0, hid)], lsem.at[7]),
     ]
     for copy in locals_:
         copy.start()
     pl.semaphore_wait(barrier, 3 * (RING - 1) + 1)
 
-    pieces = ((0, 0, hw), (1, 0, mid), (1, mid, mid), (2, 0, hw))
+    pieces = ((0, 0, hw),) + tuple((1, start, size) for start, size in CUTS) + ((2, 0, hw),)
 
     def ring_copy(which, d):
         to = (x + d) % RING
@@ -116,7 +121,7 @@
         dst = (mb.at[x], xb.at[mine, here], yb.at[mine, here])[kind]
         return remote(src, dst, ag_s.at[which * 3 + d - 1], ag_r.at[which * 3 + d - 1], dev_x(to))
 
-    rings = [[ring_copy(which, d) for d in (1, 3, 2)] for which in range(4)]
+    rings = [[ring_copy(which, d) for d in (1, 3, 2)] for which in range(len(pieces))]
 
     def start_ring(which):
         for copy in rings[which]:
@@ -126,10 +131,58 @@
         for copy in rings[which]:
             copy.wait_recv()
 
-    start_ring(0)
     start_ring(1)
     for copy in locals_:
         copy.wait()
+
+    logits = lax.dot_general(
+        ob[pl.ds(2 * tr, routes), :], xb[mine, :], NT, preferred_element_type=f32
+    ) + lax.dot_general(
+        ob[pl.ds(2 * tr + routes, routes), :], ob[pl.ds(0, tr), :], NT, preferred_element_type=f32
+    )
+    scores = jnp.exp(logits)
+    experts = 2 * COLUMNS
+    gsc[...] = routed_scale * scores[:experts] / jnp.sum(scores, axis=0, keepdims=True)
+    spread = lax.broadcasted_iota(jnp.int32, (experts, tr), 0)
+    spread = (spread % COLUMNS) * 2 + spread // COLUMNS
+    hits = jnp.zeros((experts, tr), f32)
+    for k in range(ids.shape[0]):
+        hits = hits + jnp.where(ids[k : k + 1, :] == spread, 1.0, 0.0)
+    ahead = lax.broadcasted_iota(jnp.int32, (tr, tr), 0) < lax.broadcasted_iota(jnp.int32, (tr, tr), 1)
+    rank = jnp.dot(hits.astype(bf16), jnp.where(ahead, 1.0, 0.0).astype(bf16), preferred_element_type=f32)
+    want = jnp.where((hits > 0.5) & (rank < cap), rank + (cap * x).astype(f32), -1.0)
+    ones = jnp.ones((16, tr), bf16)
+    base_here = jnp.dot(ones, xb[mine, :], preferred_element_type=f32)[0:1]
+    base_away = jnp.dot(ones, ob[pl.ds(0, tr), :], preferred_element_type=f32)[0:1]
+    words = prompt[...].astype(f32)
+    lanes = lax.broadcasted_iota(jnp.int32, (1, 2 * LANES), 1)
+    spot = lanes == col * 16 + 12 + x
+    pair = ((mate[0] // 2) * 16 + (mate[0] % 2) * 2 + x_lo).astype(f32)
+    pair = jnp.where(spot, pair, 0.0)
+    for lo in range(2):
+        base = jnp.where(x_lo == lo, base_here, base_away)
+        for hi in range(2):
+            xx = 2 * hi + lo
+            meta[xx, 0:16] = want[16 * hi : 16 * hi + 16]
+            meta[xx, 16:32] = gsc[pl.ds(hi, 16, stride=2), :]
+            for j in range(hw // LANES):
+                meta[xx, 32 + j : 33 + j] = words[:, lo * hw + j * LANES : lo * hw + (j + 1) * LANES]
+                meta[xx, 52 + j : 53 + j] = base[:, j * LANES : (j + 1) * LANES]
+            meta[xx, 72:80] = jnp.zeros((8, LANES), f32)
+            meta[xx, 72:73] = pair[:, :LANES]
+            meta[xx, 73:74] = pair[:, LANES:]
+    start_ring(0)
+    mb[x] = meta[x]
+    margin = -jnp.sum(logp[...], axis=1, keepdims=True)
+    for j in range(hw // 512):
+        lane = pl.ds(j * 512, 512)
+        both = xb[mine, lane].astype(f32) * yb[mine, lane].astype(f32)
+        both += ob[pl.ds(0, tr), lane].astype(f32) * ob[pl.ds(tr, tr), lane].astype(f32)
+        margin += jnp.sum(jnp.sum(both, axis=0, keepdims=True), axis=1, keepdims=True)
+    acc[...] = jnp.zeros_like(acc)
+    acc[0:1, :] = jnp.where(spot, -klr[0], 0.0)
+    acc[1:2, :] = jnp.where(spot, margin, 0.0)
+    acc[2:3, :] = jnp.where(spot, jnp.where(label[0] == 1, 1.0, -1.0), 0.0)
     wait_ring(0)
 
     exty[...] = jnp.zeros_like(exty)
@@ -145,9 +198,10 @@
         wd[pl.ds(hid, LANES), lane] = block.astype(bf16)
 
     def shipment(n):
-        if n < 2:
-            return rb, 0, n * mid, mid, 0, n * (mid // 2), m1x, m2x, xin
-        size, at = PARTS[n - 2], PART_AT[n - 2]
+        if n < 3:
+            start, width = CUTS[n]
+            return rb, 0, start, width, 0, start // 2, m1x, m2x, xin
+        size, at = PARTS[n - 3], PART_AT[n - 3]
         return size, at * COLUMNS, 0, hw, at * 9, 0, m1y, m2y, yin
 
     def block(n, cc):
@@ -231,8 +285,8 @@
 
     def build(n):
         size, base, start, width = shipment(n)[:4]
-        at = 0 if n < 2 else PART_AT[n - 2]
-        source = xb if n < 2 else yb
+        at = 0 if n < 3 else PART_AT[n - 3]
+        source = xb if n < 3 else yb
 
         def plane(zz):
             pick = jnp.concatenate([picks(zz * RING + i, at, size) for i in range(RING)], axis=0)
@@ -240,7 +294,7 @@
             for lo in range(start, start + width, wide):
                 lane = pl.ds(lo, min(wide, start + width - lo))
                 made = jnp.dot(pick, source[:, lane], preferred_element_type=f32)
-                if n == 4:
+                if n == 5:
                     made = made + jnp.concatenate([exty[:, lane]] * RING, axis=0)
                 ob[place_, lane] = made.astype(bf16)
             if n == 0:
@@ -285,7 +339,7 @@
 
         loop(9, go)
         loop(6, lambda i: straight(n, i).wait_send())
-        if n < 2:
+        if n < 3:
             keep(n).wait()
 
     def forwards_sent(n):
@@ -302,7 +356,7 @@
 
         loop(9, go)
         loop(6, lambda i: straight(n, i).wait_recv())
-        if n >= 2:
+        if n >= 3:
             keep(n).wait()
 
     span = 256
@@ -328,8 +382,6 @@
         ra[at, :] = part
         ras[at, :] = part.astype(bf16)
         pair_y(j).start()
-
-    acc[...] = own[...]
 
     def meet(p):
         size, at = PARTS[p], PART_AT[p]
@@ -378,27 +430,33 @@
     start_ring(3)
     build(1)
     forward(0)
+    wait_ring(3)
+    start_ring(4)
+    build(2)
+    forward(1)
     built_sent(0)
-    forward(1)
     built_sent(1)
-    wait_ring(3)
-    build(2)
+    forward(2)
+    built_sent(2)
+    wait_ring(4)
     build(3)
-    arrived(0)
-    arrived(1)
-    loop(5, use_x)
-    forward(2)
     build(4)
+    for n in range(3):
+        arrived(n)
+    loop(2, use_x)
     forward(3)
-    arrived(2)
-    loop(2, use_y)
+    loop(5, use_x, 2)
+    build(5)
     forward(4)
     arrived(3)
+    loop(2, use_y)
+    forward(5)
+    arrived(4)
     loop(4, use_y, 2)
     loop(5, lambda j: pair_x(j).wait_recv())
     loop(2, lambda j: pair_y(j).wait_recv())
     meet(0)
-    arrived(4)
+    arrived(5)
     last_at = rows(4 * span, span)
     last_part = lax.dot_general(yin[last_at, :], wd[...], NT, preferred_element_type=f32)
     ra[last_at, :] = last_part[:, :hid]
@@ -438,9 +496,9 @@
     ring_sum(0, lambda d: dev_x((x + d) % RING))
     ring_sum(1, lambda d: dev_col(plus(0, d)))
     ring_sum(2, lambda d: dev_col(plus(d, 0)))
-    for n in range(2, 5):
+    for n in range(3, 6):
         built_sent(n)
-    for n in range(5):
+    for n in range(6):
         forwards_sent(n)
     loop(5, lambda j: pair_x(j).wait_send())
     loop(5, lambda j: pair_y(j).wait_send())
@@ -474,7 +532,7 @@
         loop(COLUMNS, go)
 
     quarter = hw // 2
-    step = 256
+    step = 640
     other = (1 - core) * quarter
     this = core * quarter
     hid_t = m2y.at[pl.ds(0, hid)]
@@ -491,7 +549,7 @@
         return jnp.dot(hid_t[...], yin[:, at], preferred_element_type=f32)
 
     def piece(j, base=0):
-        return pl.ds(pl.multiple_of(base + j * step, step), step)
+        return pl.ds(pl.multiple_of(base + j * step, LANES), step)
 
     def other_up(j):
         pap[piece(j), :] = up_block(other, j).astype(bf16)
@@ -513,8 +571,8 @@
     up_copy.start()
     for p in range(3):
         scaled(ra, ras, PART_AT[p] * COLUMNS, PARTS[p], PART_AT[p])
-    for j in range(slots // step):
-        at = pl.ds(j * step, step)
+    for j in range(slots // span):
+        at = pl.ds(j * span, span)
         hid_t[:, at] = ras[at, :].T
     loop(blocks, other_down)
     down_copy.start()
@@ -544,42 +602,12 @@
     x_lo, core, x_hi, col = place()
     x = x_hi * 2 + x_lo
 
-    logits = jnp.dot(tokens, router, preferred_element_type=f32)
-    scores = jnp.exp(logits)
-    gates = routed_scale * (scores / jnp.sum(scores, axis=1, keepdims=True))[:, :experts]
-    named = jnp.any(expert_ids[:, :, None] == jnp.arange(experts, dtype=jnp.int32), axis=1)
-    before = (jnp.arange(tr)[:, None] > jnp.arange(tr)[None, :]).astype(bf16)
-    rank = jnp.dot(before, named.astype(bf16), preferred_element_type=f32)
-    want = jnp.where(named & (rank < cap), rank + (cap * x).astype(f32), -1.0)
-    by_expert = jnp.stack([want, gates]).transpose(2, 0, 1).reshape(COLUMNS, 2, 2, tr)
-    by_expert = by_expert.transpose(1, 2, 0, 3).reshape(2, 2 * COLUMNS, tr)
-
-    tokens_f = tokens.astype(f32)
-    own_margin = jnp.sum(tokens_f * readout.astype(f32)) - jnp.sum(ref_logp)
-    base = jnp.sum(tokens_f, axis=0).reshape(2, hw // LANES, LANES)
-    prompt = prompt_read.astype(f32).reshape(2, hw // LANES, LANES)
-    lane = jnp.arange(2 * LANES)
-    spot = lane == col * 16 + 12 + x
-    pair = (kl_pair[0] // 2) * 16 + (kl_pair[0] % 2) * 2 + x_lo
-    misc = jnp.pad(jnp.where(spot, pair, 0).astype(f32).reshape(2, LANES), ((0, 6), (0, 0)))
-    per_half = jnp.concatenate([prompt, base], axis=1)
-    meta = jnp.concatenate(
-        [
-            jnp.repeat(by_expert, 2, axis=0),
-            jnp.concatenate([per_half, per_half], axis=0),
-            jnp.broadcast_to(misc, (RING, 8, LANES)),
-        ],
-        axis=1,
-    )
-    sign = jnp.where(labels[0] == 1, 1.0, -1.0)
-    own = jnp.where(spot[None, :], jnp.stack([-kl_ref[0], own_margin, sign])[:, None], 0.0)
-    own = jnp.pad(own, ((0, 5), (0, 0)))
-
     slots = COLUMNS * META
     quarter = hw // 2
     dma = pltpu.SemaphoreType.DMA
     any_ = pl.BlockSpec(memory_space=pl.ANY)
     vmem = pl.BlockSpec(memory_space=pltpu.VMEM)
+    smem = pl.BlockSpec(memory_space=pltpu.SMEM)
     up, down, small = pl.pallas_call(
         functools.partial(kernel, cap, hw),
         out_shape=(
@@ -587,7 +615,7 @@
             jax.ShapeDtypeStruct((hid, quarter), bf16),
             jax.ShapeDtypeStruct((8, 2 * LANES), f32),
         ),
-        in_specs=[any_, any_, any_, vmem, any_, any_],
+        in_specs=[any_, any_, any_, vmem, vmem, vmem, smem, smem, smem, any_, any_],
         out_specs=(any_, any_, vmem),
         scratch_shapes=[
             pltpu.VMEM((RING * tr, hw), bf16),
@@ -612,14 +640,16 @@
             pltpu.VMEM((COLUMNS * 16, hid), f32),
             pltpu.VMEM((COLUMNS * 16, LANES), f32),
             pltpu.VMEM((16, hw), f32),
+            pltpu.VMEM((RING, META, LANES), f32),
+            pltpu.VMEM((2 * COLUMNS, tr), f32),
             pltpu.VMEM((8, 2 * LANES), f32),
             pltpu.VMEM((9, 8, 2 * LANES), f32),
             pltpu.VMEM((8, 2 * LANES), f32),
-            dma((5,)), dma((5,)),
-            dma((12,)), dma((12,)),
+            dma((8,)), dma((6,)),
+            dma((15,)), dma((15,)),
         ]
-        + [dma((5, 9)) for _ in range(8)]
-        + [dma((5, 6)) for _ in range(2)]
+        + [dma((6, 9)) for _ in range(8)]
+        + [dma((6, 6)) for _ in range(2)]
         + [
             dma((5,)), dma((5,)),
             dma((5,)), dma((5,)),
@@ -632,7 +662,10 @@
         ),
         cost_estimate=pl.CostEstimate(flops=40 * 10**9, bytes_accessed=30 * 10**6, transcendentals=10**6),
         name="routed_step",
-    )(tokens, readout, meta, own, w_up[0], w_down[0])
+    )(
+        tokens, readout, router.T, expert_ids.T, ref_logp.reshape(1, tr), prompt_read, labels, kl_pair, kl_ref,
+        w_up[0], w_down[0],
+    )
     here = col * 16 + 12 + x
     losses = lax.dynamic_slice(small, (0, here), (1, 1)).reshape(1)
     kl_terms = lax.dynamic_slice(small, (1, here), (1, 1)).reshape(1)

time: 256 us -> 242 us (0.945)
  other arithmetic: 6.67 us -> 0 us
  Pallas kernels: 238 us -> 234 us
    reduce_sum x2 -> x0, other arithmetic: 4.31 us -> none  [local(): own_margin = jnp.sum(tokens_f * readout.astype(f32)) - jnp.sum(ref_logp)]
    pallas_call x1, Pallas kernels: 238 us -> 234 us  [local(): pl.pallas_call(functools.partial(kernel, cap, hw), out_shape=(jax.ShapeDt...]
where the time goes in v4:
time: 242 us
  Pallas kernels  234 us (97%)
  local copies, waits for them, and re-layouts  5.7 us (2%)
  between operations  2.62 us (1%)
    pallas_call x1, Pallas kernels, local(): pl.pallas_call(functools.partial(kernel, cap, hw), out_shape=(jax.ShapeDt...  234 us

profile of v4, /device:TPU:1, one launch (start us, length us, event | category | flops | bytes accessed | tf_op | source)
XLA Modules:
  0.0 242.2 jit_solution(15593967274061312863)
XLA Ops:
  2.6 233.8 %routed_step.1 = (bf16[1280,768]{1,0:T(8,128)(2,1)}, bf16[768,1280]{1,0:T(8,128)(2,1)}, f32[8,256]{1,0:T(8,128)}) custom-call(bf16[128,5120]{1,0:T(8,128)(2,1)} %tok.1, bf16[128,5120]{1,0:T(8,128)(2,1)} %rdo.1, bf16[160,5120]{1,0:T(8,128)(2,1)} %bitcast.13, s32[6,128]{1,0:T(8,128)} %bitcast.14, f32[1,128]{1,0:T(1,128)} %bitcast.15, bf16[1,5120]{1,0:T(2,128)(2,1)} %prompt.1, ...), custom_call_target="tpu_custom_call" | custom-call | flops 40000000000 | bytes 30000000 | tf_op jit(solution)/shard_map/routed_step/pallas_call | solution.py:611
  236.5 1.3 constant_dynamic-slice_fusion
  237.8 0.0 copy-start
  237.8 3.1 %copy.20 = bf16[1,1280,768]{2,1,0:T(8,128)(2,1)} copy(bf16[1,1280,768]{2,1,0:T(8,128)(2,1)} %bitcast.10) | data formatting | bytes 3932160
  240.9 0.0 copy-done
  240.9 1.3 copy.21
Async XLA Ops:
  237.8 3.1 %copy-start = (bf16[768,1280]{1,0:T(8,128)(2,1)S(1)}, bf16[768,1280]{1,0:T(8,128)(2,1)}, u32[]{:S(2)}) copy-start(bf16[768,1280]{1,0:T(8,128)(2,1)} %get-tuple-element.8) | copy-start | bytes 5898244

commit v5 on v4

--- a/solution.py
+++ b/solution.py
@@ -42,7 +42,7 @@
     xb, yb, mb, ob, xin, yin, m1x, m2x, m1y, m2y, wu, wd, pa, ra, pas, pap, ras, rap, prs, hst, wst,
     exty, meta, gsc, acc, arb, arc,
     lsem, osem, ag_s, ag_r, a1s, a1r, a2s, a2r, b1s, b1r, b2s, b2r, ds, dr,
-    ps, pr, qs, qr, ar_s, ar_r, c_s, c_r, g_s, g_r,
+    ps, pr, qs, qr, ar_s, ar_r, g_s, g_r,
 ):
     rb = META
     tr = tok.shape[0]
@@ -56,6 +56,9 @@
     def dev_x(xx):
         return ((xx % 2) * 2 + core, col * 2 + xx // 2)
 
+    def dev_across(xx):
+        return ((xx % 2) * 2 + 1 - core, col * 2 + xx // 2)
+
     def dev_col(cc):
         return (dp, cc * 2 + x_hi)
 
@@ -89,9 +92,8 @@
         pl.semaphore_signal(barrier, inc=1, device_id=dev, device_id_type=MESH)
 
     loop(RING, lambda d: greet(dev_x((x + d) % RING)), 1)
-    loop(RING, lambda d: greet(dev_col(plus(d, 0))), 1)
-    loop(RING, lambda d: greet(dev_col(plus(0, d))), 1)
-    greet(sibling)
+    loop(RING, lambda d: greet(dev_across((x + d) % RING)))
+    loop(COLUMNS, lambda k: greet(dev_col(plus(k // RING, k % RING))), 1)
     half = pl.ds(pl.multiple_of(x_lo * hw, LANES), hw)
     away = pl.ds(pl.multiple_of((1 - x_lo) * hw, LANES), hw)
     mine = pl.ds(pl.multiple_of(x * tr, LANES), tr)
@@ -108,7 +110,7 @@
     ]
     for copy in locals_:
         copy.start()
-    pl.semaphore_wait(barrier, 3 * (RING - 1) + 1)
+    pl.semaphore_wait(barrier, 2 * RING - 1 + COLUMNS - 1)
 
     pieces = ((0, 0, hw),) + tuple((1, start, size) for start, size in CUTS) + ((2, 0, hw),)
 
@@ -132,7 +134,7 @@
             copy.wait_recv()
 
     start_ring(1)
-    for copy in locals_:
+    for copy in locals_[:6]:
         copy.wait()
 
     logits = lax.dot_general(
@@ -151,9 +153,13 @@
     ahead = lax.broadcasted_iota(jnp.int32, (tr, tr), 0) < lax.broadcasted_iota(jnp.int32, (tr, tr), 1)
     rank = jnp.dot(hits.astype(bf16), jnp.where(ahead, 1.0, 0.0).astype(bf16), preferred_element_type=f32)
     want = jnp.where((hits > 0.5) & (rank < cap), rank + (cap * x).astype(f32), -1.0)
-    ones = jnp.ones((16, tr), bf16)
-    base_here = jnp.dot(ones, xb[mine, :], preferred_element_type=f32)[0:1]
-    base_away = jnp.dot(ones, ob[pl.ds(0, tr), :], preferred_element_type=f32)[0:1]
+
+    def column_sums(ref, at):
+        parts = [ref[at, pl.ds(j * 512, 512)].astype(f32) for j in range(hw // 512)]
+        return jnp.concatenate([jnp.sum(part, axis=0, keepdims=True) for part in parts], axis=1)
+
+    base_here = column_sums(xb, mine)
+    base_away = column_sums(ob, pl.ds(0, tr))
     words = prompt[...].astype(f32)
     lanes = lax.broadcasted_iota(jnp.int32, (1, 2 * LANES), 1)
     spot = lanes == col * 16 + 12 + x
@@ -185,18 +191,6 @@
     acc[2:3, :] = jnp.where(spot, jnp.where(label[0] == 1, 1.0, -1.0), 0.0)
     wait_ring(0)
 
-    exty[...] = jnp.zeros_like(exty)
-    tall = lax.broadcasted_iota(jnp.int32, (LANES, LANES), 0)
-    for j in range(hw // LANES):
-        lane = pl.ds(j * LANES, LANES)
-        for b in range(RING):
-            exty[12 + b : 13 + b, lane] = mb[b, 32 + j : 33 + j, :]
-        terms = split3(mb[x, 52 + j : 53 + j, :]) + split3(mb[x + 1 - 2 * x_lo, 52 + j : 53 + j, :])
-        block = jnp.zeros((LANES, LANES), f32)
-        for i, term in enumerate(terms):
-            block = jnp.where(tall == i, term, block)
-        wd[pl.ds(hid, LANES), lane] = block.astype(bf16)
-
     def shipment(n):
         if n < 3:
             start, width = CUTS[n]
@@ -423,6 +417,19 @@
 
         loop(COLUMNS, go)
 
+    def side_rows():
+        exty[...] = jnp.zeros_like(exty)
+        tall = lax.broadcasted_iota(jnp.int32, (LANES, LANES), 0)
+        for j in range(hw // LANES):
+            lane = pl.ds(j * LANES, LANES)
+            for b in range(RING):
+                exty[12 + b : 13 + b, lane] = mb[b, 32 + j : 33 + j, :]
+            terms = split3(mb[x, 52 + j : 53 + j, :]) + split3(mb[x + 1 - 2 * x_lo, 52 + j : 53 + j, :])
+            block = jnp.zeros((LANES, LANES), f32)
+            for i, term in enumerate(terms):
+                block = jnp.where(tall == i, term, block)
+            wd[pl.ds(hid, LANES), lane] = block.astype(bf16)
+
     wait_ring(1)
     start_ring(2)
     build(0)
@@ -441,6 +448,9 @@
     wait_ring(4)
     build(3)
     build(4)
+    for copy in locals_[6:]:
+        copy.wait()
+    side_rows()
     for n in range(3):
         arrived(n)
     loop(2, use_x)
@@ -465,8 +475,17 @@
     wst[...] = last_part[:, hid:]
     loop(4, lambda j: pair_y(j).wait_recv(), 2)
     meet(1)
+    for n in range(3, 6):
+        built_sent(n)
+    for n in range(6):
+        forwards_sent(n)
+    loop(5, lambda j: pair_x(j).wait_send())
+    for ring in rings:
+        for copy in ring:
+            copy.wait_send()
     pair_y(4).wait_recv()
     meet(2)
+    loop(5, lambda j: pair_y(j).wait_send())
 
     wide_t = wst[...].T
     base_own = wide_t[0:1] + wide_t[1:2] + wide_t[2:3]
@@ -482,39 +501,33 @@
     chosen = jnp.where((named.astype(f32) == pairs) & used, terms, 0.0)
     acc[0:1, :] += jnp.sum(chosen, axis=0, keepdims=True)
 
-    def ring_sum(axis, dev):
-        copies = [
-            remote(acc, arb.at[axis * 3 + d - 1], ar_s.at[axis * 3 + d - 1], ar_r.at[axis * 3 + d - 1], dev(d))
-            for d in (1, 3, 2)
-        ]
-        for copy in copies:
-            copy.start()
-        for copy in copies:
-            copy.wait()
-        acc[...] = acc[...] + arb[axis * 3] + arb[axis * 3 + 1] + arb[axis * 3 + 2]
-
-    ring_sum(0, lambda d: dev_x((x + d) % RING))
-    ring_sum(1, lambda d: dev_col(plus(0, d)))
-    ring_sum(2, lambda d: dev_col(plus(d, 0)))
-    for n in range(3, 6):
-        built_sent(n)
-    for n in range(6):
-        forwards_sent(n)
-    loop(5, lambda j: pair_x(j).wait_send())
-    loop(5, lambda j: pair_y(j).wait_send())
-    for ring in rings:
-        for copy in ring:
-            copy.wait_send()
-    swap = remote(acc, arc, c_s.at[0], c_r.at[0], sibling)
-    swap.start()
-    swap.wait()
-    kl_row = jnp.where(used, acc[0:1, :], 0.0)
-    kl_other = jnp.where(used, arc[0:1, :], 0.0)
+    def along(d):
+        return remote(acc, arb.at[d - 1], ar_s.at[d - 1], ar_r.at[d - 1], dev_x((x + d) % RING))
+
+    def across(d):
+        return remote(acc, arb.at[3 + d], ar_s.at[3 + d], ar_r.at[3 + d], dev_across((x + d) % RING))
+
+    def around(k):
+        return remote(acc, arc.at[k - 1], ar_s.at[6 + k], ar_r.at[6 + k], dev_col(plus(k // RING, k % RING)))
+
+    ringed = [along(d) for d in (1, 3, 2)] + [across(d) for d in (0, 1, 3, 2)]
+    for copy in ringed:
+        copy.start()
+    for copy in ringed:
+        copy.wait()
+    acc[...] = acc[...] + arb[0] + arb[1] + arb[2]
+    acc[4:5, :] = arb[3, 0:1] + arb[4, 0:1] + arb[5, 0:1] + arb[6, 0:1]
+    loop(COLUMNS, lambda k: around(k).start(), 1)
+    loop(COLUMNS, lambda k: around(k).wait(), 1)
+    total = acc[...]
+    for k in range(COLUMNS - 1):
+        total = total + arc[k]
+    kl_row, kl_other = total[0:1], total[4:5]
     count = RING * COLUMNS * 2
     anchor = jnp.sum(kl_row + kl_other, axis=1, keepdims=True) / count
-    signed = acc[2:3, :]
-    kept = jax.nn.sigmoid(kto_beta * signed * (acc[1:2, :] - anchor))
-    slope = -loss_scale * kto_beta * signed * kept * (1.0 - kept)
+    signed = total[2:3]
+    kept = jax.nn.sigmoid(kto_beta * signed * (total[1:2] - anchor))
+    slope = -kto_beta * signed * kept * (1.0 - kept)
     small_out[...] = jnp.zeros_like(small_out)
     small_out[0:1, :] = 1.0 - kept
     small_out[1:2, :] = kl_row
@@ -643,8 +656,8 @@
             pltpu.VMEM((RING, META, LANES), f32),
             pltpu.VMEM((2 * COLUMNS, tr), f32),
             pltpu.VMEM((8, 2 * LANES), f32),
-            pltpu.VMEM((9, 8, 2 * LANES), f32),
-            pltpu.VMEM((8, 2 * LANES), f32),
+            pltpu.VMEM((2 * RING - 1, 8, 2 * LANES), f32),
+            pltpu.VMEM((COLUMNS - 1, 8, 2 * LANES), f32),
             dma((8,)), dma((6,)),
             dma((15,)), dma((15,)),
         ]
@@ -653,8 +666,7 @@
         + [
             dma((5,)), dma((5,)),
             dma((5,)), dma((5,)),
-            dma((9,)), dma((9,)),
-            dma((1,)), dma((1,)),
+            dma((22,)), dma((22,)),
             dma((2,)), dma((2,)),
         ],
         compiler_params=pltpu.CompilerParams(
@@ -669,7 +681,7 @@
     here = col * 16 + 12 + x
     losses = lax.dynamic_slice(small, (0, here), (1, 1)).reshape(1)
     kl_terms = lax.dynamic_slice(small, (1, here), (1, 1)).reshape(1)
-    return up[None], down[None], losses, kl_terms
+    return (up * bf16(loss_scale))[None], (down * bf16(loss_scale))[None], losses, kl_terms
 
 
 def solution(mesh):

time: 242 us -> 240 us (level)
  other arithmetic: 0 us -> 4.57 us
  local copies, waits for them, and re-layouts: 5.7 us -> 1.34 us
  Pallas kernels: 234 us -> 231 us
    broadcast_in_dim x0 -> x2, other arithmetic: none -> 4.57 us  [the longest x1 3.13 us: local(): (down * bf16(loss_scale))[None]]
    unnamed x4 -> x2, local copies, waits for them, and re-layouts: 4.36 us -> 0.01 us
    pallas_call x1, Pallas kernels: 234 us -> 231 us  [local(): pl.pallas_call(functools.partial(kernel, cap, hw), out_shape=(jax.ShapeDt...]
where the time goes in v5:
time: 240 us
  Pallas kernels  231 us (96%)
  other arithmetic  4.57 us (2%)
  between operations  2.62 us (1%)
    pallas_call x1, Pallas kernels, local(): pl.pallas_call(functools.partial(kernel, cap, hw), out_shape=(jax.ShapeDt...  231 us

profile of v5, /device:TPU:1, one launch (start us, length us, event | category | flops | bytes accessed | tf_op | source)
XLA Modules:
  0.0 239.8 jit_solution(15500754032816936973)
XLA Ops:
  2.6 231.3 %routed_step.1 = (bf16[1280,768]{1,0:T(8,128)(2,1)}, bf16[768,1280]{1,0:T(8,128)(2,1)}, f32[8,256]{1,0:T(8,128)}) custom-call(bf16[128,5120]{1,0:T(8,128)(2,1)} %tok.1, bf16[128,5120]{1,0:T(8,128)(2,1)} %rdo.1, bf16[160,5120]{1,0:T(8,128)(2,1)} %bitcast.13, s32[6,128]{1,0:T(8,128)} %bitcast.14, f32[1,128]{1,0:T(1,128)} %bitcast.15, bf16[1,5120]{1,0:T(2,128)(2,1)} %prompt.1, ...), custom_call_target="tpu_custom_call" | custom-call | flops 40000000000 | bytes 30000000 | tf_op jit(solution)/shard_map/routed_step/pallas_call | solution.py:624
  233.9 1.3 constant_dynamic-slice_fusion
  235.2 0.0 copy-start
  235.2 3.1 %multiply_bitcast_fusion = bf16[1,768,1280]{2,1,0:T(8,128)(2,1)} fusion(bf16[768,1280]{1,0:T(8,128)(2,1)} %get-tuple-element.8), kind=kLoop, calls=%fused_computation | loop fusion | flops 983040 | bytes 3932160 | tf_op jit(solution)/shard_map/broadcast_in_dim | solution.py:684
  238.3 0.0 copy-done
  238.3 1.4 multiply_bitcast_fusion.1
Async XLA Ops:
  235.2 3.1 %copy-start = (bf16[1280,768]{1,0:T(8,128)(2,1)S(1)}, bf16[1280,768]{1,0:T(8,128)(2,1)}, u32[]{:S(2)}) copy-start(bf16[1280,768]{1,0:T(8,128)(2,1)} %get-tuple-element.7) | copy-start | bytes 5898244
